TPU v7x, 256 devices: a whole 4x4x8 slice. The times are simulated.
256 devices in a mesh: qrow: 16 (over z_lo, x), kcol: 16 (over z_hi, y, core).
Axes of the slice: x: 4, y: 4, z: 8 (z_hi: 2, z_lo: 4; z = z_hi * 4 + z_lo), core: 2. Of those that a mesh axis runs over, the one named last changes fastest.
Arguments:
- queries: bfloat16 [1024, 8192], P(('qrow', 'kcol')), may hold values from -200 to 200
- keys_values: bfloat16 [2, 32768, 512], P(None, ('kcol', 'qrow')), may hold values from -8 to 8
- doc_blocks: int32 [256], replicated, may hold values from 0 to 11, never falling along the last dimension, each value on 1 to 129 neighbouring positions
Outputs:
- attended: bfloat16 [1024, 8192], P(('qrow', 'kcol'))
Inputs may be any that keep to these rules, and one draw needn't show every extreme that they name: doc_blocks[b] is the document of positions 128 b to 128 b + 127; each document covers 1 to 129 consecutive entries (blocks), one document exactly that many.
All inputs are finite; a program needn't handle non-finite values.
Results may differ from a plain program's by a relative error of at most 0.0046.
Values may be sent and summed in bfloat16 or wider, within the bound.
No kernel may reach another device: no remote copies, remote signals or barrier semaphores. Data moves between devices by JAX's collectives and lax.ppermute only.
A program may use at most 128 MiB of HBM per device.

v0:
```python
import math

import jax
import jax.numpy as jnp
from jax import lax
from jax.experimental import pallas as pl
from jax.experimental.pallas import tpu as pltpu
from jax.sharding import Mesh
from jax.sharding import PartitionSpec as P

HEADS = 64
GROUPS = 4
WIDTH = 128
BLOCK = 128
HEADS_PER_GROUP = HEADS // GROUPS
SLOT_ROWS = 72
ROWS = 256
KEYS = 1024
STEP = KEYS // BLOCK
MASKED = -1e30
EXP_SCALE = math.log2(math.e) / math.sqrt(WIDTH)
VMEM = pl.BlockSpec(memory_space=pltpu.VMEM)
SMEM = pl.BlockSpec(memory_space=pltpu.SMEM)
PARAMS = pltpu.CompilerParams(vmem_limit_bytes=32 * 1024 * 1024)


def three_pieces(value):
    hi = value.astype(jnp.bfloat16).astype(jnp.float32)
    rest = value - hi
    mid = rest.astype(jnp.bfloat16).astype(jnp.float32)
    return hi, mid, rest - mid


def attend(
    scal, q_ref, a0, a1, a2, a3, b0, b1, b2, b3, out_ref,
    k_scr, v_scr, acc, m_scr, l_scr, steps, s_a, s_b, p_a, p_b,
):
    zl, y, core, causal = scal[16], scal[17], scal[18], scal[19]
    for k in range(4):
        own, other = (a0, a1, a2, a3)[k], (b0, b1, b2, b3)[k]
        for s in range(4):
            at = ((y + k) & 3) * 8 + (s ^ zl)
            for src, p in ((own, at + core * 4), (other, at + (core ^ 1) * 4)):
                rows = pl.ds(pl.multiple_of(p * BLOCK, BLOCK), BLOCK)
                k_scr[rows, :] = src[s, 0]
                v_scr[rows, :] = src[s, 1]
    m_scr[...] = jnp.full_like(m_scr, MASKED)
    l_scr[...] = jnp.zeros_like(l_scr)

    def put(n, group, start, lo, slack):
        steps[0, n] = group
        steps[1, n] = start
        steps[2, n] = lo
        steps[3, n] = slack

    def plan(group, n):
        lo, hi = scal[group], scal[8 + group]
        count = (jnp.maximum(hi - lo, 0) + STEP - 1) // STEP

        @pl.when(count > 0)
        def _():
            acc[group] = jnp.zeros((WIDTH, ROWS), jnp.float32)

        def one(i, n):
            diagonal = (i == 0) & (causal == 1) & (hi == scal[20 + group])
            put(n, group, hi - STEP - STEP * i, lo, jnp.where(diagonal, 0, BLOCK))
            return n + 1

        return lax.fori_loop(0, count, one, n)

    n = lax.fori_loop(0, 8, plan, jnp.int32(0))
    key = lax.broadcasted_iota(jnp.int32, (BLOCK, ROWS), 0)
    row = lax.broadcasted_iota(jnp.int32, (1, ROWS), 1)
    query = (row >> 7) * 64 + ((row >> 6) & 1) * 32 + y * 8 + core * 4 + (row & 3)

    def scores(i, s_ref):
        group, start = steps[0, i], steps[1, i]
        keys = k_scr[pl.ds(pl.multiple_of(start * BLOCK, KEYS), KEYS), :]
        q = q_ref[pl.ds(pl.multiple_of(group * ROWS, ROWS), ROWS), :]
        s_ref[...] = lax.dot_general(
            keys, q, (((1,), (1,)), ((), ())), preferred_element_type=jnp.float32
        )

    def weigh(i, s_ref, p_ref):
        group, start, lo, slack = steps[0, i], steps[1, i], steps[2, i], steps[3, i]
        tail = slice(KEYS - BLOCK, KEYS)
        s_ref[tail, :] = jnp.where(key <= query + slack, s_ref[tail, :], MASKED)
        m_old = m_scr[group, 0:1, :]
        m_new = m_old
        bias = []
        for j in range(STEP):
            bias.append(jnp.where(start + j < lo, jnp.float32(MASKED), jnp.float32(0.0)))
            top = jnp.max(s_ref[j * BLOCK : (j + 1) * BLOCK, :], axis=0, keepdims=True)
            m_new = jnp.maximum(m_new, top + bias[j])
        total = jnp.zeros((1, ROWS), jnp.float32)
        for j in range(STEP):
            at = slice(j * BLOCK, (j + 1) * BLOCK)
            p = jnp.exp2((s_ref[at, :] - (m_new - bias[j])) * EXP_SCALE)
            total = total + jnp.sum(p, axis=0, keepdims=True)
            p_ref[at, :] = p.astype(jnp.bfloat16)
        alpha = jnp.exp2((m_old - m_new) * EXP_SCALE)
        m_scr[group, 0:1, :] = m_new
        l_scr[group, 0:1, :] = l_scr[group, 0:1, :] * alpha + total
        values = v_scr[pl.ds(pl.multiple_of(start * BLOCK, KEYS), KEYS), :]
        acc[group] = acc[group] * alpha + lax.dot_general(
            values, p_ref[...], (((0,), (0,)), ((), ())), preferred_element_type=jnp.float32
        )

    @pl.when(n > 0)
    def _():
        for extra in range(2):
            put(n + extra, steps[0, n - 1], steps[1, n - 1], 64, BLOCK)
        scores(0, s_a)

        def pair(i, carry):
            scores(2 * i + 1, s_b)
            weigh(2 * i, s_a, p_a)
            scores(2 * i + 2, s_a)
            weigh(2 * i + 1, s_b, p_b)
            return carry

        lax.fori_loop(0, (n + 1) // 2, pair, 0)

    def finish(group, carry):
        live = scal[group] < scal[8 + group]

        @pl.when(live)
        def _():
            part = acc[group].T.astype(jnp.bfloat16)
            for j in range(4):
                out_ref[group * 4 + j, 0:64, :] = part[j * 64 : (j + 1) * 64]

        @pl.when(jnp.logical_not(live))
        def _():
            for j in range(4):
                out_ref[group * 4 + j, 0:64, :] = jnp.zeros((64, WIDTH), jnp.bfloat16)

        stats = (*three_pieces(m_scr[group, 0:1, :]), *three_pieces(l_scr[group, 0:1, :]))
        stats = jnp.concatenate([*stats, jnp.zeros((2, ROWS), jnp.float32)], axis=0)
        stats = stats.astype(jnp.bfloat16)
        for j in range(4):
            out_ref[group * 4 + j, 64:72, :] = stats[:, j // 2 * 128 : (j // 2 + 1) * 128]
        return carry

    lax.fori_loop(0, 8, finish, 0)


def attend_call(scal, q, a, b):
    return pl.pallas_call(
        attend,
        out_shape=jax.ShapeDtypeStruct((32, SLOT_ROWS, WIDTH), jnp.bfloat16),
        in_specs=[SMEM] + [VMEM] * 9,
        out_specs=VMEM,
        scratch_shapes=[
            pltpu.VMEM((32 * BLOCK, WIDTH), jnp.bfloat16),
            pltpu.VMEM((32 * BLOCK, WIDTH), jnp.bfloat16),
            pltpu.VMEM((8, WIDTH, ROWS), jnp.float32),
            pltpu.VMEM((8, 8, ROWS), jnp.float32),
            pltpu.VMEM((8, 8, ROWS), jnp.float32),
            pltpu.SMEM((4, 72), jnp.int32),
            pltpu.VMEM((KEYS, ROWS), jnp.float32),
            pltpu.VMEM((KEYS, ROWS), jnp.float32),
            pltpu.VMEM((KEYS, ROWS), jnp.bfloat16),
            pltpu.VMEM((KEYS, ROWS), jnp.bfloat16),
        ],
        compiler_params=PARAMS,
        name="attend",
    )(scal, q, *a, *b)


def combine(scal, parts, out_ref):
    odd = scal[28] == 1
    lane = lax.broadcasted_iota(jnp.int32, (1, WIDTH), 1)
    pick = lax.broadcasted_iota(jnp.int32, (64, 512), 1) & 63
    pick = pick == lax.broadcasted_iota(jnp.int32, (64, 512), 0)
    for g in range(GROUPS):
        m, l = [], []
        for part in range(8):
            st = parts[g * 8 + part, 64:72, :].astype(jnp.float32)
            m.append(st[0:1] + st[1:2] + st[2:3])
            l.append(st[3:4] + st[4:5] + st[5:6])
        m, l = jnp.concatenate(m, axis=0), jnp.concatenate(l, axis=0)
        w = jnp.exp2((m - jnp.max(m, axis=0, keepdims=True)) * EXP_SCALE)
        w = w / jnp.sum(w * l, axis=0, keepdims=True)
        turned_w = pltpu.roll(w, 64, 1)
        low, high = jnp.where(odd, turned_w, w), jnp.where(odd, w, turned_w)
        line = [jnp.where(lane < 64, low[p : p + 1], high[p + 1 : p + 2]) for p in (0, 2, 4, 6)]
        line = jnp.concatenate(line, axis=1)
        both = jnp.concatenate([parts[g * 8 + part, 0:64, :] for part in range(8)], axis=0)
        total = jnp.zeros((64, WIDTH), jnp.float32)
        for piece in three_pieces(line):
            spread = jnp.where(pick, jnp.broadcast_to(piece, (64, 512)), 0.0)
            total = total + jnp.dot(
                spread.astype(jnp.bfloat16), both, preferred_element_type=jnp.float32
            )
        for h in range(HEADS_PER_GROUP):
            at = (g * HEADS_PER_GROUP + h) * WIDTH
            out_ref[:, at : at + WIDTH] = total[h * 4 : (h + 1) * 4, :].astype(jnp.bfloat16)


def turned(k):
    return [((i + k) % 4, i) for i in range(4)]


def per_device(queries, keys_values, doc_blocks):
    zl, x, zh, y, core = (lax.axis_index(a) for a in ("zl", "x", "zh", "y", "core"))
    parts = ("zl", "x", "zh")
    q = queries.reshape(4, GROUPS, HEADS_PER_GROUP, WIDTH).transpose(1, 2, 0, 3)
    q = q.reshape(GROUPS, 1, 64, WIDTH)
    q = jnp.broadcast_to(q, (GROUPS, 8, 64, WIDTH)).reshape(32, 64, WIDTH)
    q = lax.all_to_all(q, parts, 0, 0, tiled=True).reshape(2048, WIDTH)
    pieces = []
    for s in range(4):
        piece = lax.dynamic_slice_in_dim(keys_values, (zl ^ s) * WIDTH, WIDTH, 2)
        pieces.append(lax.ppermute(piece, "zl", [(i, i ^ s) for i in range(4)]) if s else piece)
    a0 = jnp.stack(pieces)
    a1, a2, a3 = (lax.ppermute(a0, "y", turned(k)) for k in (1, 2, 3))
    swap = [(0, 1), (1, 0)]
    b0 = lax.ppermute(a0, "core", swap)
    b1 = lax.ppermute(a1, "core", swap)
    b3 = lax.ppermute(a3, "core", swap)
    a2, b3 = lax.optimization_barrier((a2, b3))
    b = [b0, b1, lax.ppermute(a2, "core", swap), b3]
    query_block = jnp.arange(8, dtype=jnp.int32)
    at = query_block * 32 + 31
    index = jnp.arange(256, dtype=jnp.int32)
    own_doc = jnp.sum(jnp.where(index[None] == at[:, None], doc_blocks[None], 0), axis=1)
    start = jnp.sum((doc_blocks[None] < own_doc[:, None]).astype(jnp.int32), axis=1)
    lo = jnp.clip((start - x - 128 * zh + 3) >> 2, 0, 32)
    end = 8 * (query_block + 1) - 32 * zh
    mine = jnp.stack([zl, y, core, (x == 3).astype(jnp.int32)]).astype(jnp.int32)
    scal = jnp.concatenate([lo, jnp.clip(end, 0, 32), mine, end, zh[None]]).astype(jnp.int32)

    part = attend_call(scal, q, (a0, a1, a2, a3), b)
    part = lax.all_to_all(part, parts, 0, 0, tiled=True)
    return pl.pallas_call(
        combine,
        out_shape=jax.ShapeDtypeStruct((4, HEADS * WIDTH), jnp.bfloat16),
        in_specs=[SMEM, VMEM],
        out_specs=VMEM,
        compiler_params=PARAMS,
        name="combine",
    )(scal, part)


def solution(mesh):
    split = Mesh(mesh.devices.reshape(4, 4, 2, 4, 2), ("zl", "x", "zh", "y", "core"))
    in_specs = (
        P(("zl", "x", "zh", "y", "core"), None),
        P(None, ("zh", "y", "core", "zl", "x"), None),
        P(),
    )
    out_specs = P(("zl", "x", "zh", "y", "core"), None)
    return jax.shard_map(
        per_device, mesh=split, in_specs=in_specs, out_specs=out_specs, check_vma=False
    )
```

profile of v0, /device:TPU:32, one launch (start us, length us, event | category | flops | bytes accessed | tf_op | source)
XLA Modules:
  0.0 68.8 jit_solution(10135683408833459299)
XLA Ops:
  0.0 1.0 %dynamic-slice_bitcast_fusion = (bf16[1,2,128,128]{3,2,1,0:T(8,128)(2,1)S(1)}, bf16[2,128,128]{2,1,0:T(8,128)(2,1)S(1)}, bf16[2,128,128]{2,1,0:T(8,128)(2,1)S(1)}, bf16[2,128,128]{2,1,0:T(8,128)(2,1)S(1)}) fusion(bf16[2,128,512]{2,1,0:T(8,128)(2,1)} %param.4, s32[]{:T(128)S(6)} %select_n.17, s32[]{:T(128)S(6)} %select_n.18, s32[]{:T(128)S(6)} %select_n.20, ...), kind=kLoop, calls=%fused_computation.1 | loop fusion | bytes 524304 | tf_op jit(solution)/shard_map/stack | solution.py:216
  1.0 1.9 %collective-permute-start = (bf16[2,128,128]{2,1,0:T(8,128)(2,1)S(1)}, bf16[2,128,128]{2,1,0:T(8,128)(2,1)S(1)}, u32[]{:S(2)}, u32[]{:S(2)}) collective-permute-start(bf16[2,128,128]{2,1,0:T(8,128)(2,1)S(1)} %get-tuple-element.10), channel_id=1, source_target_pairs={{0,64},{64,0},{128,192},{192,128},{1,65},{65,1},{129,193},{193,129... | collective-permute-start | bytes 196616 | tf_op jit(solution)/shard_map/ppermute | solution.py:215
  2.9 2.0 %collective-permute-start.2 = (bf16[2,128,128]{2,1,0:T(8,128)(2,1)S(1)}, bf16[2,128,128]{2,1,0:T(8,128)(2,1)S(1)}, u32[]{:S(2)}, u32[]{:S(2)}) collective-permute-start(bf16[2,128,128]{2,1,0:T(8,128)(2,1)S(1)} %get-tuple-element.11), channel_id=1, source_target_pairs={{0,192},{64,128},{128,64},{192,0},{1,193},{65,129},{129,65},{193,1... | collective-permute-start | bytes 196616 | tf_op jit(solution)/shard_map/ppermute | solution.py:215
  4.9 0.6 collective-permute-start.1
  5.5 0.0 copy-done
  5.5 0.9 %broadcast_in_dim.28 = bf16[4,8,64,128]{3,2,1,0:T(8,128)(2,1)} broadcast(bf16[4,64,128]{2,1,0:T(8,128)(2,1)S(1)} %bitcast.18), dimensions={0,2,3} | broadcast | bytes 589824 | tf_op jit(solution)/shard_map/broadcast_in_dim | solution.py:210
  6.4 10.7 %all-to-all-start = ((bf16[32,64,128]{2,1,0:T(8,128)(2,1)}), bf16[32,64,128]{2,1,0:T(8,128)(2,1)S(1)}, u32[]{:S(2)}, u32[]{:S(2)}) async-start(bf16[32,64,128]{2,1,0:T(8,128)(2,1)} %bitcast.8), calls=%async_computation | async-start | bytes 1048576 | tf_op jit(solution)/shard_map/all_to_all | solution.py:211
  17.1 0.0 collective-permute-done
  17.2 0.0 collective-permute-done.2
  17.2 0.0 collective-permute-done.1
  17.2 1.7 %collective-permute-start.5 = (bf16[4,2,128,128]{3,2,1,0:T(8,128)(2,1)S(1)}, bf16[4,2,128,128]{3,2,1,0:T(8,128)(2,1)S(1)}, u32[]{:S(2)}, u32[]{:S(2)}) collective-permute-start(bf16[4,2,128,128]{3,2,1,0:T(8,128)(2,1)S(1)} %pad_maximum_fusion.a0), channel_id=1, source_target_pairs={{6,0},{0,2},{2,4},{4,6},{7,1},{1,3},{3,5},{5,7},{14,8},{8,10},{10,... | collective-permute-start | bytes 786440 | tf_op jit(solution)/shard_map/ppermute | solution.py:217
  18.9 2.9 %collective-permute-start.4 = (bf16[4,2,128,128]{3,2,1,0:T(8,128)(2,1)S(1)}, bf16[4,2,128,128]{3,2,1,0:T(8,128)(2,1)S(1)}, u32[]{:S(2)}, u32[]{:S(2)}) collective-permute-start(bf16[4,2,128,128]{3,2,1,0:T(8,128)(2,1)S(1)} %pad_maximum_fusion.a0), channel_id=1, source_target_pairs={{4,0},{6,2},{0,4},{2,6},{5,1},{7,3},{1,5},{3,7},{12,8},{14,10},{8,... | collective-permute-start | bytes 786440 | tf_op jit(solution)/shard_map/ppermute | solution.py:217
  21.8 1.3 %collective-permute-start.3 = (bf16[4,2,128,128]{3,2,1,0:T(8,128)(2,1)S(1)}, bf16[4,2,128,128]{3,2,1,0:T(8,128)(2,1)S(1)}, u32[]{:S(2)}, u32[]{:S(2)}) collective-permute-start(bf16[4,2,128,128]{3,2,1,0:T(8,128)(2,1)S(1)} %pad_maximum_fusion.a0), channel_id=1, source_target_pairs={{2,0},{4,2},{6,4},{0,6},{3,1},{5,3},{7,5},{1,7},{10,8},{12,10},{14... | collective-permute-start | bytes 786440 | tf_op jit(solution)/shard_map/ppermute | solution.py:217
  23.1 3.5 %collective-permute-done.5.a3 = bf16[4,2,128,128]{3,2,1,0:T(8,128)(2,1)S(1)} collective-permute-done((bf16[4,2,128,128]{3,2,1,0:T(8,128)(2,1)S(1)}, bf16[4,2,128,128]{3,2,1,0:T(8,128)(2,1)S(1)}, u32[]{:S(2)}, u32[]{:S(2)}) %collective-permute-start.5) | collective-permute-done | bytes 262176 | tf_op jit(solution)/shard_map/ppermute | solution.py:217
  26.6 0.0 collective-permute-start.6
  26.6 0.7 copy-done.1
  27.3 0.2 select_reduce_fusion
  27.5 0.2 convert_reduce_fusion
  27.7 0.6 collective-permute-start.7
  28.3 3.2 %collective-permute-done.3.a1 = bf16[4,2,128,128]{3,2,1,0:T(8,128)(2,1)S(1)} collective-permute-done((bf16[4,2,128,128]{3,2,1,0:T(8,128)(2,1)S(1)}, bf16[4,2,128,128]{3,2,1,0:T(8,128)(2,1)S(1)}, u32[]{:S(2)}, u32[]{:S(2)}) %collective-permute-start.3) | collective-permute-done | bytes 262176 | tf_op jit(solution)/shard_map/ppermute | solution.py:217
  31.5 0.0 collective-permute-start.8
  31.5 0.5 collective-permute-done.4.a2
  32.0 0.0 collective-permute-done.6.b3
  32.0 0.0 collective-permute-start.9
  32.1 0.1 concatenate.3.scal
  32.1 0.0 collective-permute-done.7.b0
  32.1 0.9 %collective-permute-done.8.b1 = bf16[4,2,128,128]{3,2,1,0:T(8,128)(2,1)S(1)} collective-permute-done((bf16[4,2,128,128]{3,2,1,0:T(8,128)(2,1)S(1)}, bf16[4,2,128,128]{3,2,1,0:T(8,128)(2,1)S(1)}, u32[]{:S(2)}, u32[]{:S(2)}) %collective-permute-start.8) | collective-permute-done | bytes 262176 | tf_op jit(solution)/shard_map/ppermute | solution.py:220
  33.0 0.5 collective-permute-done.9.b2
  33.6 0.9 %all-to-all-done = bf16[32,64,128]{2,1,0:T(8,128)(2,1)S(1)} async-done(((bf16[32,64,128]{2,1,0:T(8,128)(2,1)}), bf16[32,64,128]{2,1,0:T(8,128)(2,1)S(1)}, u32[]{:S(2)}, u32[]{:S(2)}) %all-to-all-start) | async-done | bytes 524320 | tf_op jit(solution)/shard_map/all_to_all | solution.py:211
  34.5 6.2 %attend.1 = bf16[32,72,128]{2,1,0:T(8,128)(2,1)S(1)} custom-call(s32[29]{0:T(128)S(1)} %concatenate.3.scal, bf16[2048,128]{1,0:T(8,128)(2,1)S(1)} %bitcast.17, bf16[4,2,128,128]{3,2,1,0:T(8,128)(2,1)S(1)} %pad_maximum_fusion.a0, bf16[4,2,128,128]{3,2,1,0:T(8,128)(2,1)S(1)} %collective-permute-done.3.a1, ...), custom_call_target="tpu_custom_call" | custom-call | tf_op jit(solution)/shard_map/attend/pallas_call | solution.py:149
  40.7 26.5 %all_to_all.10.parts = bf16[32,72,128]{2,1,0:T(8,128)(2,1)S(1)} all-to-all(bf16[32,72,128]{2,1,0:T(8,128)(2,1)S(1)} %attend.1), channel_id=1, replica_groups=mesh['zl'=4,'x'=4,'zh'=2,'y'=4,'core'=2] {'zl','x','zh'}, dimensions={0} | all-to-all | bytes 1179648 | tf_op jit(solution)/shard_map/all_to_all | solution.py:235
  67.2 1.6 %combine.1 = bf16[4,8192]{1,0:T(4,128)(2,1)} custom-call(s32[29]{0:T(128)S(1)} %concatenate.3.scal, bf16[32,72,128]{2,1,0:T(8,128)(2,1)S(1)} %all_to_all.10.parts), custom_call_target="tpu_custom_call" | custom-call | tf_op jit(solution)/shard_map/combine/pallas_call | solution.py:236
  (6 shorter events, 0.1 us)
Async XLA Ops:
  0.0 5.5 %copy-start = (bf16[4,8192]{1,0:T(4,128)(2,1)S(1)}, bf16[4,8192]{1,0:T(4,128)(2,1)}, u32[]{:S(2)}) copy-start(bf16[4,8192]{1,0:T(4,128)(2,1)} %param.3) | copy-start | bytes 196612
  1.0 16.1 %collective-permute-start = (bf16[2,128,128]{2,1,0:T(8,128)(2,1)S(1)}, bf16[2,128,128]{2,1,0:T(8,128)(2,1)S(1)}, u32[]{:S(2)}, u32[]{:S(2)}) collective-permute-start(bf16[2,128,128]{2,1,0:T(8,128)(2,1)S(1)} %get-tuple-element.10), channel_id=1, source_target_pairs={{0,64},{64,0},{128,192},{192,128},{1,65},{65,1},{129,193},{193,129... | collective-permute-start | bytes 196616 | tf_op jit(solution)/shard_map/ppermute | solution.py:215
  2.9 14.2 %collective-permute-start.2 = (bf16[2,128,128]{2,1,0:T(8,128)(2,1)S(1)}, bf16[2,128,128]{2,1,0:T(8,128)(2,1)S(1)}, u32[]{:S(2)}, u32[]{:S(2)}) collective-permute-start(bf16[2,128,128]{2,1,0:T(8,128)(2,1)S(1)} %get-tuple-element.11), channel_id=1, source_target_pairs={{0,192},{64,128},{128,64},{192,0},{1,193},{65,129},{129,65},{193,1... | collective-permute-start | bytes 196616 | tf_op jit(solution)/shard_map/ppermute | solution.py:215
  4.9 12.2 %collective-permute-start.1 = (bf16[2,128,128]{2,1,0:T(8,128)(2,1)S(1)}, bf16[2,128,128]{2,1,0:T(8,128)(2,1)S(1)}, u32[]{:S(2)}, u32[]{:S(2)}) collective-permute-start(bf16[2,128,128]{2,1,0:T(8,128)(2,1)S(1)} %get-tuple-element.12), channel_id=1, source_target_pairs={{0,128},{64,192},{128,0},{192,64},{1,129},{65,193},{129,1},{193,65... | collective-permute-start | bytes 196616 | tf_op jit(solution)/shard_map/ppermute | solution.py:215
  6.4 28.1 %all-to-all-start = ((bf16[32,64,128]{2,1,0:T(8,128)(2,1)}), bf16[32,64,128]{2,1,0:T(8,128)(2,1)S(1)}, u32[]{:S(2)}, u32[]{:S(2)}) async-start(bf16[32,64,128]{2,1,0:T(8,128)(2,1)} %bitcast.8), calls=%async_computation | async-start | bytes 1048576 | tf_op jit(solution)/shard_map/all_to_all | solution.py:211
  17.2 9.4 %collective-permute-start.5 = (bf16[4,2,128,128]{3,2,1,0:T(8,128)(2,1)S(1)}, bf16[4,2,128,128]{3,2,1,0:T(8,128)(2,1)S(1)}, u32[]{:S(2)}, u32[]{:S(2)}) collective-permute-start(bf16[4,2,128,128]{3,2,1,0:T(8,128)(2,1)S(1)} %pad_maximum_fusion.a0), channel_id=1, source_target_pairs={{6,0},{0,2},{2,4},{4,6},{7,1},{1,3},{3,5},{5,7},{14,8},{8,10},{10,... | collective-permute-start | bytes 786440 | tf_op jit(solution)/shard_map/ppermute | solution.py:217
  18.9 13.1 %collective-permute-start.4 = (bf16[4,2,128,128]{3,2,1,0:T(8,128)(2,1)S(1)}, bf16[4,2,128,128]{3,2,1,0:T(8,128)(2,1)S(1)}, u32[]{:S(2)}, u32[]{:S(2)}) collective-permute-start(bf16[4,2,128,128]{3,2,1,0:T(8,128)(2,1)S(1)} %pad_maximum_fusion.a0), channel_id=1, source_target_pairs={{4,0},{6,2},{0,4},{2,6},{5,1},{7,3},{1,5},{3,7},{12,8},{14,10},{8,... | collective-permute-start | bytes 786440 | tf_op jit(solution)/shard_map/ppermute | solution.py:217
  21.8 9.7 %collective-permute-start.3 = (bf16[4,2,128,128]{3,2,1,0:T(8,128)(2,1)S(1)}, bf16[4,2,128,128]{3,2,1,0:T(8,128)(2,1)S(1)}, u32[]{:S(2)}, u32[]{:S(2)}) collective-permute-start(bf16[4,2,128,128]{3,2,1,0:T(8,128)(2,1)S(1)} %pad_maximum_fusion.a0), channel_id=1, source_target_pairs={{2,0},{4,2},{6,4},{0,6},{3,1},{5,3},{7,5},{1,7},{10,8},{12,10},{14... | collective-permute-start | bytes 786440 | tf_op jit(solution)/shard_map/ppermute | solution.py:217
  26.6 5.4 %collective-permute-start.6 = (bf16[4,2,128,128]{3,2,1,0:T(8,128)(2,1)S(1)}, bf16[4,2,128,128]{3,2,1,0:T(8,128)(2,1)S(1)}, u32[]{:S(2)}, u32[]{:S(2)}) collective-permute-start(bf16[4,2,128,128]{3,2,1,0:T(8,128)(2,1)S(1)} %collective-permute-done.5.a3), channel_id=1, source_target_pairs={{0,1},{1,0},{2,3},{3,2},{4,5},{5,4},{6,7},{7,6},{8,9},{9,8},{10,11... | collective-permute-start | bytes 786440 | tf_op jit(solution)/shard_map/ppermute | solution.py:221
  26.6 0.7 copy-start.1
  27.7 4.5 %collective-permute-start.7 = (bf16[4,2,128,128]{3,2,1,0:T(8,128)(2,1)S(1)}, bf16[4,2,128,128]{3,2,1,0:T(8,128)(2,1)S(1)}, u32[]{:S(2)}, u32[]{:S(2)}) collective-permute-start(bf16[4,2,128,128]{3,2,1,0:T(8,128)(2,1)S(1)} %pad_maximum_fusion.a0), channel_id=1, source_target_pairs={{0,1},{1,0},{2,3},{3,2},{4,5},{5,4},{6,7},{7,6},{8,9},{9,8},{10,11... | collective-permute-start | bytes 786440 | tf_op jit(solution)/shard_map/ppermute | solution.py:219
  31.5 1.5 %collective-permute-start.8 = (bf16[4,2,128,128]{3,2,1,0:T(8,128)(2,1)S(1)}, bf16[4,2,128,128]{3,2,1,0:T(8,128)(2,1)S(1)}, u32[]{:S(2)}, u32[]{:S(2)}) collective-permute-start(bf16[4,2,128,128]{3,2,1,0:T(8,128)(2,1)S(1)} %collective-permute-done.3.a1), channel_id=1, source_target_pairs={{0,1},{1,0},{2,3},{3,2},{4,5},{5,4},{6,7},{7,6},{8,9},{9,8},{10,11... | collective-permute-start | bytes 786440 | tf_op jit(solution)/shard_map/ppermute | solution.py:220
  32.0 1.5 %collective-permute-start.9 = (bf16[4,2,128,128]{3,2,1,0:T(8,128)(2,1)S(1)}, bf16[4,2,128,128]{3,2,1,0:T(8,128)(2,1)S(1)}, u32[]{:S(2)}, u32[]{:S(2)}) collective-permute-start(bf16[4,2,128,128]{3,2,1,0:T(8,128)(2,1)S(1)} %collective-permute-done.4.a2), channel_id=1, source_target_pairs={{0,1},{1,0},{2,3},{3,2},{4,5},{5,4},{6,7},{7,6},{8,9},{9,8},{10,11... | collective-permute-start | bytes 786440 | tf_op jit(solution)/shard_map/ppermute | solution.py:223
where the time goes:
time: 69.3 us; the launch traced here: 68.8 us
  blocking collectives  26.5 us (38%)
  starting transfers between devices  21.7 us (31%)
  waiting for transfers between devices  9.56 us (14%)
  Pallas kernels  7.87 us (11%)
  local copies, waits for them, and re-layouts  2.67 us (4%)
    all_to_all x1, blocking collectives, per_device(): part = lax.all_to_all(part, parts, 0, 0, tiled=True)  26.5 us
    all_to_all x1, starting transfers between devices, per_device(): q = lax.all_to_all(q, parts, 0, 0, tiled=True).reshape(2048, WIDTH)  10.7 us
    ppermute x3, waiting for transfers between devices, per_device(): a1, a2, a3 = (lax.ppermute(a0, 'y', turned(k)) for k in (1, 2, 3))  7.24 us
    pallas_call x1, Pallas kernels, attend_call(): pl.pallas_call(attend, out_shape=jax.ShapeDtypeStruct((32, SLOT_ROWS, WID...  6.23 us
    ppermute x3, starting transfers between devices, per_device(): a1, a2, a3 = (lax.ppermute(a0, 'y', turned(k)) for k in (1, 2, 3))  5.9 us
    ppermute x3, starting transfers between devices, per_device(): lax.ppermute(piece, 'zl', [(i, i ^ s) for i in range(4)])  4.47 us
    pallas_call x1, Pallas kernels, per_device(): pl.pallas_call(combine, out_shape=jax.ShapeDtypeStruct((4, HEADS * WIDTH)...  1.64 us
  transfers between devices with their start and end apart: 11, of which 6 were waited for; matrix products, arithmetic and copies ran while one was open for 2% of the time, Pallas kernels for 0%

commit v1 on v0

--- a/solution.py
+++ b/solution.py
@@ -31,9 +31,14 @@
     return hi, mid, rest - mid
 
 
+def statistics(m, l):
+    rows = (*three_pieces(m), *three_pieces(l), jnp.zeros((2, WIDTH), jnp.float32))
+    return jnp.concatenate(rows, axis=0).astype(jnp.bfloat16)
+
+
 def attend(
-    scal, q_ref, a0, a1, a2, a3, b0, b1, b2, b3, out_ref,
-    k_scr, v_scr, acc, m_scr, l_scr, steps, s_a, s_b, p_a, p_b,
+    scal, q0, q1, q2, q3, a0, a1, a2, a3, b0, b1, b2, b3, o0, o1, o2, o3,
+    q_ref, k_scr, v_scr, acc, m_scr, l_scr, steps, s_a, s_b, p_a, p_b,
 ):
     zl, y, core, causal = scal[16], scal[17], scal[18], scal[19]
     for k in range(4):
@@ -44,6 +49,11 @@
                 rows = pl.ds(pl.multiple_of(p * BLOCK, BLOCK), BLOCK)
                 k_scr[rows, :] = src[s, 0]
                 v_scr[rows, :] = src[s, 1]
+    for k in range(4):
+        x_at = (scal[29] + k) & 3
+        for src in range(8):
+            slot = src // 2 * 8 + x_at * 2 + src % 2
+            q_ref[pl.ds(pl.multiple_of(slot * 64, 64), 64), :] = (q0, q1, q2, q3)[k][src]
     m_scr[...] = jnp.full_like(m_scr, MASKED)
     l_scr[...] = jnp.zeros_like(l_scr)
 
@@ -121,37 +131,41 @@
 
         lax.fori_loop(0, (n + 1) // 2, pair, 0)
 
-    def finish(group, carry):
-        live = scal[group] < scal[8 + group]
-
-        @pl.when(live)
-        def _():
-            part = acc[group].T.astype(jnp.bfloat16)
-            for j in range(4):
-                out_ref[group * 4 + j, 0:64, :] = part[j * 64 : (j + 1) * 64]
-
-        @pl.when(jnp.logical_not(live))
-        def _():
-            for j in range(4):
-                out_ref[group * 4 + j, 0:64, :] = jnp.zeros((64, WIDTH), jnp.bfloat16)
-
-        stats = (*three_pieces(m_scr[group, 0:1, :]), *three_pieces(l_scr[group, 0:1, :]))
-        stats = jnp.concatenate([*stats, jnp.zeros((2, ROWS), jnp.float32)], axis=0)
-        stats = stats.astype(jnp.bfloat16)
-        for j in range(4):
-            out_ref[group * 4 + j, 64:72, :] = stats[:, j // 2 * 128 : (j // 2 + 1) * 128]
-        return carry
-
-    lax.fori_loop(0, 8, finish, 0)
+    for k, out_ref in enumerate((o0, o1, o2, o3)):
+        x_at = (scal[29] + k) & 3
+        lanes = pl.ds(pl.multiple_of((x_at & 1) * 128, 128), 128)
+
+        def finish(zl_at, carry, out_ref=out_ref, x_at=x_at, lanes=lanes):
+            group = 2 * zl_at + (x_at >> 1)
+            live = scal[group] < scal[8 + group]
+
+            @pl.when(live)
+            def _():
+                part = acc[group, :, lanes].T.astype(jnp.bfloat16)
+                for j in range(2):
+                    out_ref[zl_at * 2 + j, 0:64, :] = part[j * 64 : (j + 1) * 64]
+
+            @pl.when(jnp.logical_not(live))
+            def _():
+                for j in range(2):
+                    out_ref[zl_at * 2 + j, 0:64, :] = jnp.zeros((64, WIDTH), jnp.bfloat16)
+
+            stats = statistics(m_scr[group, 0:1, lanes], l_scr[group, 0:1, lanes])
+            for j in range(2):
+                out_ref[zl_at * 2 + j, 64:72, :] = stats
+            return carry
+
+        lax.fori_loop(0, 4, finish, 0)
 
 
 def attend_call(scal, q, a, b):
     return pl.pallas_call(
         attend,
-        out_shape=jax.ShapeDtypeStruct((32, SLOT_ROWS, WIDTH), jnp.bfloat16),
-        in_specs=[SMEM] + [VMEM] * 9,
-        out_specs=VMEM,
+        out_shape=(jax.ShapeDtypeStruct((8, SLOT_ROWS, WIDTH), jnp.bfloat16),) * 4,
+        in_specs=[SMEM] + [VMEM] * 12,
+        out_specs=(VMEM,) * 4,
         scratch_shapes=[
+            pltpu.VMEM((2048, WIDTH), jnp.bfloat16),
             pltpu.VMEM((32 * BLOCK, WIDTH), jnp.bfloat16),
             pltpu.VMEM((32 * BLOCK, WIDTH), jnp.bfloat16),
             pltpu.VMEM((8, WIDTH, ROWS), jnp.float32),
@@ -165,34 +179,54 @@
         ],
         compiler_params=PARAMS,
         name="attend",
-    )(scal, q, *a, *b)
+    )(scal, *q, *a, *b)
+
+
+def weights(stats):
+    stats = [st.astype(jnp.float32) for st in stats]
+    m = jnp.concatenate([st[0:1] + st[1:2] + st[2:3] for st in stats], axis=0)
+    l = jnp.concatenate([st[3:4] + st[4:5] + st[5:6] for st in stats], axis=0)
+    top = jnp.max(m, axis=0, keepdims=True)
+    w = jnp.exp2((m - top) * EXP_SCALE)
+    return top, w, jnp.sum(w * l, axis=0, keepdims=True)
+
+
+def weighed(line, pick, rows):
+    total = jnp.zeros((pick.shape[0], WIDTH), jnp.float32)
+    for piece in three_pieces(line):
+        spread = jnp.where(pick, jnp.broadcast_to(piece, pick.shape), 0.0).astype(jnp.bfloat16)
+        total = total + jnp.dot(spread, rows, preferred_element_type=jnp.float32)
+    return total
+
+
+def merge(p0, p1, p2, p3, out_ref):
+    parts = (p0, p1, p2, p3)
+    pick = lax.broadcasted_iota(jnp.int32, (128, 512), 1) & 127
+    pick = pick == lax.broadcasted_iota(jnp.int32, (128, 512), 0)
+    for zl_at in range(4):
+        top, w, l = weights([part[2 * zl_at, 64:72, :] for part in parts])
+        line = jnp.concatenate([w[k : k + 1] for k in range(4)], axis=1)
+        rows = [part[2 * zl_at + j, 0:64, :] for part in parts for j in range(2)]
+        total = weighed(line, pick, jnp.concatenate(rows, axis=0)).astype(jnp.bfloat16)
+        stats = statistics(top, l)
+        for j in range(2):
+            out_ref[2 * zl_at + j, 0:64, :] = total[j * 64 : (j + 1) * 64]
+            out_ref[2 * zl_at + j, 64:72, :] = stats
 
 
 def combine(scal, parts, out_ref):
     odd = scal[28] == 1
     lane = lax.broadcasted_iota(jnp.int32, (1, WIDTH), 1)
-    pick = lax.broadcasted_iota(jnp.int32, (64, 512), 1) & 63
-    pick = pick == lax.broadcasted_iota(jnp.int32, (64, 512), 0)
+    pick = lax.broadcasted_iota(jnp.int32, (64, WIDTH), 1) & 63
+    pick = pick == lax.broadcasted_iota(jnp.int32, (64, WIDTH), 0)
     for g in range(GROUPS):
-        m, l = [], []
-        for part in range(8):
-            st = parts[g * 8 + part, 64:72, :].astype(jnp.float32)
-            m.append(st[0:1] + st[1:2] + st[2:3])
-            l.append(st[3:4] + st[4:5] + st[5:6])
-        m, l = jnp.concatenate(m, axis=0), jnp.concatenate(l, axis=0)
-        w = jnp.exp2((m - jnp.max(m, axis=0, keepdims=True)) * EXP_SCALE)
-        w = w / jnp.sum(w * l, axis=0, keepdims=True)
+        _, w, l = weights([parts[g * 2 + j, 64:72, :] for j in range(2)])
+        w = w / l
         turned_w = pltpu.roll(w, 64, 1)
         low, high = jnp.where(odd, turned_w, w), jnp.where(odd, w, turned_w)
-        line = [jnp.where(lane < 64, low[p : p + 1], high[p + 1 : p + 2]) for p in (0, 2, 4, 6)]
-        line = jnp.concatenate(line, axis=1)
-        both = jnp.concatenate([parts[g * 8 + part, 0:64, :] for part in range(8)], axis=0)
-        total = jnp.zeros((64, WIDTH), jnp.float32)
-        for piece in three_pieces(line):
-            spread = jnp.where(pick, jnp.broadcast_to(piece, (64, 512)), 0.0)
-            total = total + jnp.dot(
-                spread.astype(jnp.bfloat16), both, preferred_element_type=jnp.float32
-            )
+        line = jnp.where(lane < 64, low[0:1], high[1:2])
+        rows = jnp.concatenate([parts[g * 2 + j, 0:64, :] for j in range(2)], axis=0)
+        total = weighed(line, pick, rows)
         for h in range(HEADS_PER_GROUP):
             at = (g * HEADS_PER_GROUP + h) * WIDTH
             out_ref[:, at : at + WIDTH] = total[h * 4 : (h + 1) * 4, :].astype(jnp.bfloat16)
@@ -204,11 +238,11 @@
 
 def per_device(queries, keys_values, doc_blocks):
     zl, x, zh, y, core = (lax.axis_index(a) for a in ("zl", "x", "zh", "y", "core"))
-    parts = ("zl", "x", "zh")
     q = queries.reshape(4, GROUPS, HEADS_PER_GROUP, WIDTH).transpose(1, 2, 0, 3)
     q = q.reshape(GROUPS, 1, 64, WIDTH)
-    q = jnp.broadcast_to(q, (GROUPS, 8, 64, WIDTH)).reshape(32, 64, WIDTH)
-    q = lax.all_to_all(q, parts, 0, 0, tiled=True).reshape(2048, WIDTH)
+    q = jnp.broadcast_to(q, (GROUPS, 2, 64, WIDTH)).reshape(8, 64, WIDTH)
+    q = lax.all_to_all(q, ("zl", "zh"), 0, 0, tiled=True)
+    q = [q, *(lax.ppermute(q, "x", turned(k)) for k in (1, 2, 3))]
     pieces = []
     for s in range(4):
         piece = lax.dynamic_slice_in_dim(keys_values, (zl ^ s) * WIDTH, WIDTH, 2)
@@ -219,7 +253,6 @@
     b0 = lax.ppermute(a0, "core", swap)
     b1 = lax.ppermute(a1, "core", swap)
     b3 = lax.ppermute(a3, "core", swap)
-    a2, b3 = lax.optimization_barrier((a2, b3))
     b = [b0, b1, lax.ppermute(a2, "core", swap), b3]
     query_block = jnp.arange(8, dtype=jnp.int32)
     at = query_block * 32 + 31
@@ -229,10 +262,19 @@
     lo = jnp.clip((start - x - 128 * zh + 3) >> 2, 0, 32)
     end = 8 * (query_block + 1) - 32 * zh
     mine = jnp.stack([zl, y, core, (x == 3).astype(jnp.int32)]).astype(jnp.int32)
-    scal = jnp.concatenate([lo, jnp.clip(end, 0, 32), mine, end, zh[None]]).astype(jnp.int32)
+    scal = jnp.concatenate([lo, jnp.clip(end, 0, 32), mine, end, zh[None], x[None]]).astype(jnp.int32)
 
     part = attend_call(scal, q, (a0, a1, a2, a3), b)
-    part = lax.all_to_all(part, parts, 0, 0, tiled=True)
+    part = [part[0], *(lax.ppermute(part[k], "x", turned(4 - k)) for k in (1, 2, 3))]
+    part = pl.pallas_call(
+        merge,
+        out_shape=jax.ShapeDtypeStruct((8, SLOT_ROWS, WIDTH), jnp.bfloat16),
+        in_specs=[VMEM] * 4,
+        out_specs=VMEM,
+        compiler_params=PARAMS,
+        name="merge",
+    )(*part)
+    part = lax.all_to_all(part, ("zl", "zh"), 0, 0, tiled=True)
     return pl.pallas_call(
         combine,
         out_shape=jax.ShapeDtypeStruct((4, HEADS * WIDTH), jnp.bfloat16),

time: 69.3 us -> 68 us (0.981); the launches traced: 68.8 us -> 68.4 us
  blocking collectives: 26.5 us -> 14.8 us
  starting transfers between devices: 21.7 us -> 32.9 us
  waiting for transfers between devices: 9.56 us -> 13.4 us
  Pallas kernels: 7.87 us -> 5.07 us
  local copies, waits for them, and re-layouts: 2.67 us -> 1.75 us
    ppermute x0 -> x6, starting transfers between devices: none -> 13.7 us  [the longest x3 7.91 us: per_device(): lax.ppermute(part[k], 'x', turned(4 - k))]
    all_to_all x1, blocking collectives: 26.5 us -> 14.8 us  [per_device(): part = lax.all_to_all(part, ('zl', 'zh'), 0, 0, tiled=True)]
    ppermute x0 -> x6, waiting for transfers between devices: none -> 7.03 us  [the longest x3 7.02 us: per_device(): lax.ppermute(part[k], 'x', turned(4 - k))]
    ppermute x3, waiting for transfers between devices: 7.24 us -> 3.41 us  [per_device(): a1, a2, a3 = (lax.ppermute(a0, 'y', turned(k)) for k in (1, 2, 3))]
    pallas_call x1 -> x2, Pallas kernels: 6.23 us -> 3.57 us  [the longest x1 2.97 us: attend_call(): pl.pallas_call(attend, out_shape=(jax.ShapeDtypeStruct((8, SLOT_ROWS, WID...]
    all_to_all x1, starting transfers between devices: 10.7 us -> 8.13 us  [per_device(): q = lax.all_to_all(q, ('zl', 'zh'), 0, 0, tiled=True)]
    ppermute x1, waiting for transfers between devices: 0.01 us -> 0.81 us  [per_device(): b3 = lax.ppermute(a3, 'core', swap)]
  transfers between devices with their start and end apart: 11 -> 17, of which waited for: 6 -> 7; matrix products, arithmetic and copies ran while one was open for 2% -> 2% of each run, Pallas kernels for 0% -> 0%
where the time goes in v1:
time: 68 us; the launch traced here: 68.4 us
  starting transfers between devices  32.9 us (48%)
  blocking collectives  14.8 us (22%)
  waiting for transfers between devices  13.4 us (20%)
  Pallas kernels  5.07 us (7%)
  local copies, waits for them, and re-layouts  1.75 us (3%)
    all_to_all x1, blocking collectives, per_device(): part = lax.all_to_all(part, ('zl', 'zh'), 0, 0, tiled=True)  14.8 us
    all_to_all x1, starting transfers between devices, per_device(): q = lax.all_to_all(q, ('zl', 'zh'), 0, 0, tiled=True)  8.13 us
    ppermute x3, starting transfers between devices, per_device(): lax.ppermute(part[k], 'x', turned(4 - k))  7.91 us
    ppermute x3, waiting for transfers between devices, per_device(): lax.ppermute(part[k], 'x', turned(4 - k))  7.02 us
    ppermute x3, starting transfers between devices, per_device(): a1, a2, a3 = (lax.ppermute(a0, 'y', turned(k)) for k in (1, 2, 3))  5.9 us
    ppermute x3, starting transfers between devices, per_device(): q = [q, *(lax.ppermute(q, 'x', turned(k)) for k in (1, 2, 3))]  5.74 us
    ppermute x3, starting transfers between devices, per_device(): lax.ppermute(piece, 'zl', [(i, i ^ s) for i in range(4)])  4.47 us
    ppermute x3, waiting for transfers between devices, per_device(): a1, a2, a3 = (lax.ppermute(a0, 'y', turned(k)) for k in (1, 2, 3))  3.41 us
  transfers between devices with their start and end apart: 17, of which 7 were waited for; matrix products, arithmetic and copies ran while one was open for 2% of the time, Pallas kernels for 0%

profile of v1, /device:TPU:32, one launch (start us, length us, event | category | flops | bytes accessed | tf_op | source)
XLA Modules:
  0.0 68.4 jit_solution(5273847680848663997)
XLA Ops:
  0.0 1.0 %dynamic-slice_bitcast_fusion = (bf16[1,2,128,128]{3,2,1,0:T(8,128)(2,1)S(1)}, bf16[2,128,128]{2,1,0:T(8,128)(2,1)S(1)}, bf16[2,128,128]{2,1,0:T(8,128)(2,1)S(1)}, bf16[2,128,128]{2,1,0:T(8,128)(2,1)S(1)}) fusion(bf16[2,128,512]{2,1,0:T(8,128)(2,1)} %param.4, s32[]{:T(128)S(6)} %select_n.17, s32[]{:T(128)S(6)} %select_n.18, s32[]{:T(128)S(6)} %select_n.20, ...), kind=kLoop, calls=%fused_computation.1 | loop fusion | bytes 524304 | tf_op jit(solution)/shard_map/stack | solution.py:250
  1.0 1.9 %collective-permute-start.3 = (bf16[2,128,128]{2,1,0:T(8,128)(2,1)S(1)}, bf16[2,128,128]{2,1,0:T(8,128)(2,1)S(1)}, u32[]{:S(2)}, u32[]{:S(2)}) collective-permute-start(bf16[2,128,128]{2,1,0:T(8,128)(2,1)S(1)} %get-tuple-element.14), channel_id=1, source_target_pairs={{0,64},{64,0},{128,192},{192,128},{1,65},{65,1},{129,193},{193,129... | collective-permute-start | bytes 196616 | tf_op jit(solution)/shard_map/ppermute | solution.py:249
  2.9 2.0 %collective-permute-start.5 = (bf16[2,128,128]{2,1,0:T(8,128)(2,1)S(1)}, bf16[2,128,128]{2,1,0:T(8,128)(2,1)S(1)}, u32[]{:S(2)}, u32[]{:S(2)}) collective-permute-start(bf16[2,128,128]{2,1,0:T(8,128)(2,1)S(1)} %get-tuple-element.15), channel_id=1, source_target_pairs={{0,192},{64,128},{128,64},{192,0},{1,193},{65,129},{129,65},{193,1... | collective-permute-start | bytes 196616 | tf_op jit(solution)/shard_map/ppermute | solution.py:249
  4.9 0.6 collective-permute-start.4
  5.5 0.7 broadcast_in_dim.32
  6.1 8.1 %all-to-all-start = ((bf16[8,64,128]{2,1,0:T(8,128)(2,1)}), bf16[8,64,128]{2,1,0:T(8,128)(2,1)S(1)}, u32[]{:S(2)}, u32[]{:S(2)}) async-start(bf16[8,64,128]{2,1,0:T(8,128)(2,1)} %bitcast.9), calls=%async_computation | async-start | bytes 262144 | tf_op jit(solution)/shard_map/all_to_all | solution.py:244
  14.3 0.0 copy-start.1
  14.3 0.1 collective-permute-start.9
  14.4 1.7 %collective-permute-start.8 = (bf16[4,2,128,128]{3,2,1,0:T(8,128)(2,1)S(1)}, bf16[4,2,128,128]{3,2,1,0:T(8,128)(2,1)S(1)}, u32[]{:S(2)}, u32[]{:S(2)}) collective-permute-start(bf16[4,2,128,128]{3,2,1,0:T(8,128)(2,1)S(1)} %pad_maximum_fusion.a0), channel_id=1, source_target_pairs={{6,0},{0,2},{2,4},{4,6},{7,1},{1,3},{3,5},{5,7},{14,8},{8,10},{10,... | collective-permute-start | bytes 786440 | tf_op jit(solution)/shard_map/ppermute | solution.py:251
  16.1 2.9 %collective-permute-start.7 = (bf16[4,2,128,128]{3,2,1,0:T(8,128)(2,1)S(1)}, bf16[4,2,128,128]{3,2,1,0:T(8,128)(2,1)S(1)}, u32[]{:S(2)}, u32[]{:S(2)}) collective-permute-start(bf16[4,2,128,128]{3,2,1,0:T(8,128)(2,1)S(1)} %pad_maximum_fusion.a0), channel_id=1, source_target_pairs={{4,0},{6,2},{0,4},{2,6},{5,1},{7,3},{1,5},{3,7},{12,8},{14,10},{8,... | collective-permute-start | bytes 786440 | tf_op jit(solution)/shard_map/ppermute | solution.py:251
  19.0 1.3 %collective-permute-start.6 = (bf16[4,2,128,128]{3,2,1,0:T(8,128)(2,1)S(1)}, bf16[4,2,128,128]{3,2,1,0:T(8,128)(2,1)S(1)}, u32[]{:S(2)}, u32[]{:S(2)}) collective-permute-start(bf16[4,2,128,128]{3,2,1,0:T(8,128)(2,1)S(1)} %pad_maximum_fusion.a0), channel_id=1, source_target_pairs={{2,0},{4,2},{6,4},{0,6},{3,1},{5,3},{7,5},{1,7},{10,8},{12,10},{14... | collective-permute-start | bytes 786440 | tf_op jit(solution)/shard_map/ppermute | solution.py:251
  20.4 1.4 %all-to-all-done.q0 = bf16[8,64,128]{2,1,0:T(8,128)(2,1)S(1)} async-done(((bf16[8,64,128]{2,1,0:T(8,128)(2,1)}), bf16[8,64,128]{2,1,0:T(8,128)(2,1)S(1)}, u32[]{:S(2)}, u32[]{:S(2)}) %all-to-all-start) | async-done | bytes 131104 | tf_op jit(solution)/shard_map/all_to_all | solution.py:244
  21.7 1.5 %collective-permute-start.2 = (bf16[8,64,128]{2,1,0:T(8,128)(2,1)S(1)}, bf16[8,64,128]{2,1,0:T(8,128)(2,1)S(1)}, u32[]{:S(2)}, u32[]{:S(2)}) collective-permute-start(bf16[8,64,128]{2,1,0:T(8,128)(2,1)S(1)} %all-to-all-done.q0), channel_id=1, source_target_pairs={{48,0},{0,16},{16,32},{32,48},{49,1},{1,17},{17,33},{33,49},{50,2}... | collective-permute-start | bytes 393224 | tf_op jit(solution)/shard_map/ppermute | solution.py:245
  23.2 0.2 select_reduce_fusion
  23.4 0.2 convert_reduce_fusion
  23.6 2.8 %collective-permute-start.1 = (bf16[8,64,128]{2,1,0:T(8,128)(2,1)S(1)}, bf16[8,64,128]{2,1,0:T(8,128)(2,1)S(1)}, u32[]{:S(2)}, u32[]{:S(2)}) collective-permute-start(bf16[8,64,128]{2,1,0:T(8,128)(2,1)S(1)} %all-to-all-done.q0), channel_id=1, source_target_pairs={{32,0},{48,16},{0,32},{16,48},{33,1},{49,17},{1,33},{17,49},{34,2}... | collective-permute-start | bytes 393224 | tf_op jit(solution)/shard_map/ppermute | solution.py:245
  26.4 1.4 %collective-permute-start = (bf16[8,64,128]{2,1,0:T(8,128)(2,1)S(1)}, bf16[8,64,128]{2,1,0:T(8,128)(2,1)S(1)}, u32[]{:S(2)}, u32[]{:S(2)}) collective-permute-start(bf16[8,64,128]{2,1,0:T(8,128)(2,1)S(1)} %all-to-all-done.q0), channel_id=1, source_target_pairs={{16,0},{32,16},{48,32},{0,48},{17,1},{33,17},{49,33},{1,49},{18,2}... | collective-permute-start | bytes 393224 | tf_op jit(solution)/shard_map/ppermute | solution.py:245
  27.8 3.4 %collective-permute-done.7.a2 = bf16[4,2,128,128]{3,2,1,0:T(8,128)(2,1)S(1)} collective-permute-done((bf16[4,2,128,128]{3,2,1,0:T(8,128)(2,1)S(1)}, bf16[4,2,128,128]{3,2,1,0:T(8,128)(2,1)S(1)}, u32[]{:S(2)}, u32[]{:S(2)}) %collective-permute-start.7) | collective-permute-done | bytes 262176 | tf_op jit(solution)/shard_map/ppermute | solution.py:251
  31.2 0.5 collective-permute-start.11
  31.8 0.1 collective-permute-start.10
  31.9 0.1 concatenate.3.scal
  32.0 0.8 %collective-permute-done.12.b3 = bf16[4,2,128,128]{3,2,1,0:T(8,128)(2,1)S(1)} collective-permute-done((bf16[4,2,128,128]{3,2,1,0:T(8,128)(2,1)S(1)}, bf16[4,2,128,128]{3,2,1,0:T(8,128)(2,1)S(1)}, u32[]{:S(2)}, u32[]{:S(2)}) %collective-permute-start.12) | collective-permute-done | bytes 262176 | tf_op jit(solution)/shard_map/ppermute | solution.py:255
  32.8 0.4 collective-permute-done.11.b2
  33.2 0.4 collective-permute-done.10.b1
  33.5 3.0 %attend.1 = (bf16[8,72,128]{2,1,0:T(8,128)(2,1)S(1)}, bf16[8,72,128]{2,1,0:T(8,128)(2,1)S(1)}, bf16[8,72,128]{2,1,0:T(8,128)(2,1)S(1)}, bf16[8,72,128]{2,1,0:T(8,128)(2,1)S(1)}) custom-call(s32[30]{0:T(128)S(1)} %concatenate.3.scal, bf16[8,64,128]{2,1,0:T(8,128)(2,1)S(1)} %all-to-all-done.q0, bf16[8,64,128]{2,1,0:T(8,128)(2,1)S(1)} %collective-permute-done.q1, ...), custom_call_target="tpu_custom_call" | custom-call | tf_op jit(solution)/shard_map/attend/pallas_call | solution.py:162
  36.5 1.6 %collective-permute-start.13 = (bf16[8,72,128]{2,1,0:T(8,128)(2,1)S(1)}, bf16[8,72,128]{2,1,0:T(8,128)(2,1)S(1)}, u32[]{:S(2)}, u32[]{:S(2)}) collective-permute-start(bf16[8,72,128]{2,1,0:T(8,128)(2,1)S(1)} %get-tuple-element.10), channel_id=1, source_target_pairs={{48,0},{0,16},{16,32},{32,48},{49,1},{1,17},{17,33},{33,49},{50,2}... | collective-permute-start | bytes 442376 | tf_op jit(solution)/shard_map/ppermute | solution.py:268
  38.1 6.3 %collective-permute-start.14 = (bf16[8,72,128]{2,1,0:T(8,128)(2,1)S(1)}, bf16[8,72,128]{2,1,0:T(8,128)(2,1)S(1)}, u32[]{:S(2)}, u32[]{:S(2)}) collective-permute-start(bf16[8,72,128]{2,1,0:T(8,128)(2,1)S(1)} %get-tuple-element.11), channel_id=1, source_target_pairs={{32,0},{48,16},{0,32},{16,48},{33,1},{49,17},{1,33},{17,49},{34,2}... | collective-permute-start | bytes 442376 | tf_op jit(solution)/shard_map/ppermute | solution.py:268
  44.4 2.7 %collective-permute-done.13.p1 = bf16[8,72,128]{2,1,0:T(8,128)(2,1)S(1)} collective-permute-done((bf16[8,72,128]{2,1,0:T(8,128)(2,1)S(1)}, bf16[8,72,128]{2,1,0:T(8,128)(2,1)S(1)}, u32[]{:S(2)}, u32[]{:S(2)}) %collective-permute-start.13) | collective-permute-done | bytes 147488 | tf_op jit(solution)/shard_map/ppermute | solution.py:268
  47.1 4.3 %collective-permute-done.14.p2 = bf16[8,72,128]{2,1,0:T(8,128)(2,1)S(1)} collective-permute-done((bf16[8,72,128]{2,1,0:T(8,128)(2,1)S(1)}, bf16[8,72,128]{2,1,0:T(8,128)(2,1)S(1)}, u32[]{:S(2)}, u32[]{:S(2)}) %collective-permute-start.14) | collective-permute-done | bytes 147488 | tf_op jit(solution)/shard_map/ppermute | solution.py:268
  51.4 0.6 merge.1
  52.0 14.8 %all_to_all.10.parts = bf16[8,72,128]{2,1,0:T(8,128)(2,1)S(1)} all-to-all(bf16[8,72,128]{2,1,0:T(8,128)(2,1)S(1)} %merge.1), channel_id=1, replica_groups=mesh['zl'=4,'x'=4,'zh'=2,'y'=4,'core'=2] {'zl','zh'}, dimensions={0} | all-to-all | bytes 294912 | tf_op jit(solution)/shard_map/all_to_all | solution.py:277
  66.8 1.5 %combine.1 = bf16[4,8192]{1,0:T(4,128)(2,1)} custom-call(s32[30]{0:T(128)S(1)} %concatenate.3.scal, bf16[8,72,128]{2,1,0:T(8,128)(2,1)S(1)} %all_to_all.10.parts), custom_call_target="tpu_custom_call" | custom-call | tf_op jit(solution)/shard_map/combine/pallas_call | solution.py:278
  (19 shorter events, 0.1 us)
Async XLA Ops:
  0.0 5.5 %copy-start = (bf16[4,8192]{1,0:T(4,128)(2,1)S(1)}, bf16[4,8192]{1,0:T(4,128)(2,1)}, u32[]{:S(2)}) copy-start(bf16[4,8192]{1,0:T(4,128)(2,1)} %param.3) | copy-start | bytes 196612
  1.0 13.3 %collective-permute-start.3 = (bf16[2,128,128]{2,1,0:T(8,128)(2,1)S(1)}, bf16[2,128,128]{2,1,0:T(8,128)(2,1)S(1)}, u32[]{:S(2)}, u32[]{:S(2)}) collective-permute-start(bf16[2,128,128]{2,1,0:T(8,128)(2,1)S(1)} %get-tuple-element.14), channel_id=1, source_target_pairs={{0,64},{64,0},{128,192},{192,128},{1,65},{65,1},{129,193},{193,129... | collective-permute-start | bytes 196616 | tf_op jit(solution)/shard_map/ppermute | solution.py:249
  2.9 11.3 %collective-permute-start.5 = (bf16[2,128,128]{2,1,0:T(8,128)(2,1)S(1)}, bf16[2,128,128]{2,1,0:T(8,128)(2,1)S(1)}, u32[]{:S(2)}, u32[]{:S(2)}) collective-permute-start(bf16[2,128,128]{2,1,0:T(8,128)(2,1)S(1)} %get-tuple-element.15), channel_id=1, source_target_pairs={{0,192},{64,128},{128,64},{192,0},{1,193},{65,129},{129,65},{193,1... | collective-permute-start | bytes 196616 | tf_op jit(solution)/shard_map/ppermute | solution.py:249
  4.9 9.4 %collective-permute-start.4 = (bf16[2,128,128]{2,1,0:T(8,128)(2,1)S(1)}, bf16[2,128,128]{2,1,0:T(8,128)(2,1)S(1)}, u32[]{:S(2)}, u32[]{:S(2)}) collective-permute-start(bf16[2,128,128]{2,1,0:T(8,128)(2,1)S(1)} %get-tuple-element.16), channel_id=1, source_target_pairs={{0,128},{64,192},{128,0},{192,64},{1,129},{65,193},{129,1},{193,65... | collective-permute-start | bytes 196616 | tf_op jit(solution)/shard_map/ppermute | solution.py:249
  6.1 15.6 %all-to-all-start = ((bf16[8,64,128]{2,1,0:T(8,128)(2,1)}), bf16[8,64,128]{2,1,0:T(8,128)(2,1)S(1)}, u32[]{:S(2)}, u32[]{:S(2)}) async-start(bf16[8,64,128]{2,1,0:T(8,128)(2,1)} %bitcast.9), calls=%async_computation | async-start | bytes 262144 | tf_op jit(solution)/shard_map/all_to_all | solution.py:244
  14.3 8.9 %copy-start.1 = (s32[256]{0:T(256)S(1)}, s32[256]{0:T(256)}, u32[]{:S(2)}) copy-start(s32[256]{0:T(256)} %param.5) | copy-start | bytes 3076
  14.3 9.2 %collective-permute-start.9 = (bf16[4,2,128,128]{3,2,1,0:T(8,128)(2,1)S(1)}, bf16[4,2,128,128]{3,2,1,0:T(8,128)(2,1)S(1)}, u32[]{:S(2)}, u32[]{:S(2)}) collective-permute-start(bf16[4,2,128,128]{3,2,1,0:T(8,128)(2,1)S(1)} %pad_maximum_fusion.a0), channel_id=1, source_target_pairs={{0,1},{1,0},{2,3},{3,2},{4,5},{5,4},{6,7},{7,6},{8,9},{9,8},{10,11... | collective-permute-start | bytes 786440 | tf_op jit(solution)/shard_map/ppermute | solution.py:253
  14.4 12.0 %collective-permute-start.8 = (bf16[4,2,128,128]{3,2,1,0:T(8,128)(2,1)S(1)}, bf16[4,2,128,128]{3,2,1,0:T(8,128)(2,1)S(1)}, u32[]{:S(2)}, u32[]{:S(2)}) collective-permute-start(bf16[4,2,128,128]{3,2,1,0:T(8,128)(2,1)S(1)} %pad_maximum_fusion.a0), channel_id=1, source_target_pairs={{6,0},{0,2},{2,4},{4,6},{7,1},{1,3},{3,5},{5,7},{14,8},{8,10},{10,... | collective-permute-start | bytes 786440 | tf_op jit(solution)/shard_map/ppermute | solution.py:251
  16.1 15.1 %collective-permute-start.7 = (bf16[4,2,128,128]{3,2,1,0:T(8,128)(2,1)S(1)}, bf16[4,2,128,128]{3,2,1,0:T(8,128)(2,1)S(1)}, u32[]{:S(2)}, u32[]{:S(2)}) collective-permute-start(bf16[4,2,128,128]{3,2,1,0:T(8,128)(2,1)S(1)} %pad_maximum_fusion.a0), channel_id=1, source_target_pairs={{4,0},{6,2},{0,4},{2,6},{5,1},{7,3},{1,5},{3,7},{12,8},{14,10},{8,... | collective-permute-start | bytes 786440 | tf_op jit(solution)/shard_map/ppermute | solution.py:251
  19.0 12.2 %collective-permute-start.6 = (bf16[4,2,128,128]{3,2,1,0:T(8,128)(2,1)S(1)}, bf16[4,2,128,128]{3,2,1,0:T(8,128)(2,1)S(1)}, u32[]{:S(2)}, u32[]{:S(2)}) collective-permute-start(bf16[4,2,128,128]{3,2,1,0:T(8,128)(2,1)S(1)} %pad_maximum_fusion.a0), channel_id=1, source_target_pairs={{2,0},{4,2},{6,4},{0,6},{3,1},{5,3},{7,5},{1,7},{10,8},{12,10},{14... | collective-permute-start | bytes 786440 | tf_op jit(solution)/shard_map/ppermute | solution.py:251
  21.7 10.0 %collective-permute-start.2 = (bf16[8,64,128]{2,1,0:T(8,128)(2,1)S(1)}, bf16[8,64,128]{2,1,0:T(8,128)(2,1)S(1)}, u32[]{:S(2)}, u32[]{:S(2)}) collective-permute-start(bf16[8,64,128]{2,1,0:T(8,128)(2,1)S(1)} %all-to-all-done.q0), channel_id=1, source_target_pairs={{48,0},{0,16},{16,32},{32,48},{49,1},{1,17},{17,33},{33,49},{50,2}... | collective-permute-start | bytes 393224 | tf_op jit(solution)/shard_map/ppermute | solution.py:245
  23.6 8.4 %collective-permute-start.1 = (bf16[8,64,128]{2,1,0:T(8,128)(2,1)S(1)}, bf16[8,64,128]{2,1,0:T(8,128)(2,1)S(1)}, u32[]{:S(2)}, u32[]{:S(2)}) collective-permute-start(bf16[8,64,128]{2,1,0:T(8,128)(2,1)S(1)} %all-to-all-done.q0), channel_id=1, source_target_pairs={{32,0},{48,16},{0,32},{16,48},{33,1},{49,17},{1,33},{17,49},{34,2}... | collective-permute-start | bytes 393224 | tf_op jit(solution)/shard_map/ppermute | solution.py:245
  26.4 5.6 %collective-permute-start = (bf16[8,64,128]{2,1,0:T(8,128)(2,1)S(1)}, bf16[8,64,128]{2,1,0:T(8,128)(2,1)S(1)}, u32[]{:S(2)}, u32[]{:S(2)}) collective-permute-start(bf16[8,64,128]{2,1,0:T(8,128)(2,1)S(1)} %all-to-all-done.q0), channel_id=1, source_target_pairs={{16,0},{32,16},{48,32},{0,48},{17,1},{33,17},{49,33},{1,49},{18,2}... | collective-permute-start | bytes 393224 | tf_op jit(solution)/shard_map/ppermute | solution.py:245
  31.2 1.5 %collective-permute-start.12 = (bf16[4,2,128,128]{3,2,1,0:T(8,128)(2,1)S(1)}, bf16[4,2,128,128]{3,2,1,0:T(8,128)(2,1)S(1)}, u32[]{:S(2)}, u32[]{:S(2)}) collective-permute-start(bf16[4,2,128,128]{3,2,1,0:T(8,128)(2,1)S(1)} %collective-permute-done.8.a3), channel_id=1, source_target_pairs={{0,1},{1,0},{2,3},{3,2},{4,5},{5,4},{6,7},{7,6},{8,9},{9,8},{10,11... | collective-permute-start | bytes 786440 | tf_op jit(solution)/shard_map/ppermute | solution.py:255
  31.2 1.9 %collective-permute-start.11 = (bf16[4,2,128,128]{3,2,1,0:T(8,128)(2,1)S(1)}, bf16[4,2,128,128]{3,2,1,0:T(8,128)(2,1)S(1)}, u32[]{:S(2)}, u32[]{:S(2)}) collective-permute-start(bf16[4,2,128,128]{3,2,1,0:T(8,128)(2,1)S(1)} %collective-permute-done.7.a2), channel_id=1, source_target_pairs={{0,1},{1,0},{2,3},{3,2},{4,5},{5,4},{6,7},{7,6},{8,9},{9,8},{10,11... | collective-permute-start | bytes 786440 | tf_op jit(solution)/shard_map/ppermute | solution.py:256
  31.8 1.8 %collective-permute-start.10 = (bf16[4,2,128,128]{3,2,1,0:T(8,128)(2,1)S(1)}, bf16[4,2,128,128]{3,2,1,0:T(8,128)(2,1)S(1)}, u32[]{:S(2)}, u32[]{:S(2)}) collective-permute-start(bf16[4,2,128,128]{3,2,1,0:T(8,128)(2,1)S(1)} %collective-permute-done.6.a1), channel_id=1, source_target_pairs={{0,1},{1,0},{2,3},{3,2},{4,5},{5,4},{6,7},{7,6},{8,9},{9,8},{10,11... | collective-permute-start | bytes 786440 | tf_op jit(solution)/shard_map/ppermute | solution.py:254
  36.5 10.6 %collective-permute-start.13 = (bf16[8,72,128]{2,1,0:T(8,128)(2,1)S(1)}, bf16[8,72,128]{2,1,0:T(8,128)(2,1)S(1)}, u32[]{:S(2)}, u32[]{:S(2)}) collective-permute-start(bf16[8,72,128]{2,1,0:T(8,128)(2,1)S(1)} %get-tuple-element.10), channel_id=1, source_target_pairs={{48,0},{0,16},{16,32},{32,48},{49,1},{1,17},{17,33},{33,49},{50,2}... | collective-permute-start | bytes 442376 | tf_op jit(solution)/shard_map/ppermute | solution.py:268
  38.1 13.4 %collective-permute-start.14 = (bf16[8,72,128]{2,1,0:T(8,128)(2,1)S(1)}, bf16[8,72,128]{2,1,0:T(8,128)(2,1)S(1)}, u32[]{:S(2)}, u32[]{:S(2)}) collective-permute-start(bf16[8,72,128]{2,1,0:T(8,128)(2,1)S(1)} %get-tuple-element.11), channel_id=1, source_target_pairs={{32,0},{48,16},{0,32},{16,48},{33,1},{49,17},{1,33},{17,49},{34,2}... | collective-permute-start | bytes 442376 | tf_op jit(solution)/shard_map/ppermute | solution.py:268
  44.4 7.0 %collective-permute-start.15 = (bf16[8,72,128]{2,1,0:T(8,128)(2,1)S(1)}, bf16[8,72,128]{2,1,0:T(8,128)(2,1)S(1)}, u32[]{:S(2)}, u32[]{:S(2)}) collective-permute-start(bf16[8,72,128]{2,1,0:T(8,128)(2,1)S(1)} %get-tuple-element.12), channel_id=1, source_target_pairs={{16,0},{32,16},{48,32},{0,48},{17,1},{33,17},{49,33},{1,49},{18,2}... | collective-permute-start | bytes 442376 | tf_op jit(solution)/shard_map/ppermute | solution.py:268

commit v2 on v1

--- a/solution.py
+++ b/solution.py
@@ -250,10 +250,8 @@
     a0 = jnp.stack(pieces)
     a1, a2, a3 = (lax.ppermute(a0, "y", turned(k)) for k in (1, 2, 3))
     swap = [(0, 1), (1, 0)]
-    b0 = lax.ppermute(a0, "core", swap)
-    b1 = lax.ppermute(a1, "core", swap)
-    b3 = lax.ppermute(a3, "core", swap)
-    b = [b0, b1, lax.ppermute(a2, "core", swap), b3]
+    late, a3 = lax.optimization_barrier((a0, a3))
+    b = [lax.ppermute(a, "core", swap) for a in (late, a1, a2, a3)]
     query_block = jnp.arange(8, dtype=jnp.int32)
     at = query_block * 32 + 31
     index = jnp.arange(256, dtype=jnp.int32)

time: 68 us -> 66.1 us (0.972)
  the two profiles are of different devices: /device:TPU:32 before, /device:TPU:2 now
where the time goes in v2:
time: 66.1 us; the launch traced here: 64.9 us
  starting transfers between devices  28.9 us (44%)
  blocking collectives  12.5 us (19%)
  waiting for transfers between devices  12.2 us (18%)
  Pallas kernels  9.05 us (14%)
  local copies, waits for them, and re-layouts  1.75 us (3%)
    all_to_all x1, blocking collectives, per_device(): part = lax.all_to_all(part, ('zl', 'zh'), 0, 0, tiled=True)  12.5 us
    all_to_all x1, starting transfers between devices, per_device(): q = lax.all_to_all(q, ('zl', 'zh'), 0, 0, tiled=True)  7.22 us
    pallas_call x1, Pallas kernels, attend_call(): pl.pallas_call(attend, out_shape=(jax.ShapeDtypeStruct((8, SLOT_ROWS, WID...  6.96 us
    ppermute x3, waiting for transfers between devices, per_device(): lax.ppermute(part[k], 'x', turned(4 - k))  6.48 us
    ppermute x3, starting transfers between devices, per_device(): a1, a2, a3 = (lax.ppermute(a0, 'y', turned(k)) for k in (1, 2, 3))  5.9 us
    ppermute x3, starting transfers between devices, per_device(): lax.ppermute(piece, 'zl', [(i, i ^ s) for i in range(4)])  5.28 us
    ppermute x3, starting transfers between devices, per_device(): q = [q, *(lax.ppermute(q, 'x', turned(k)) for k in (1, 2, 3))]  4.83 us
    ppermute x3, starting transfers between devices, per_device(): lax.ppermute(part[k], 'x', turned(4 - k))  4.82 us
  transfers between devices with their start and end apart: 17, of which 9 were waited for; matrix products, arithmetic and copies ran while one was open for 2% of the time, Pallas kernels for 0%

profile of v2, /device:TPU:2, one launch (start us, length us, event | category | flops | bytes accessed | tf_op | source)
XLA Modules:
  0.0 64.9 jit_solution(4260956968089039332)
XLA Ops:
  0.0 1.0 %dynamic-slice_bitcast_fusion = (bf16[1,2,128,128]{3,2,1,0:T(8,128)(2,1)S(1)}, bf16[2,128,128]{2,1,0:T(8,128)(2,1)S(1)}, bf16[2,128,128]{2,1,0:T(8,128)(2,1)S(1)}, bf16[2,128,128]{2,1,0:T(8,128)(2,1)S(1)}) fusion(bf16[2,128,512]{2,1,0:T(8,128)(2,1)} %param.4, s32[]{:T(128)S(6)} %select_n.17, s32[]{:T(128)S(6)} %select_n.18, s32[]{:T(128)S(6)} %select_n.20, ...), kind=kLoop, calls=%fused_computation.1 | loop fusion | bytes 524304 | tf_op jit(solution)/shard_map/stack | solution.py:250
  1.0 2.0 %collective-permute-start.3 = (bf16[2,128,128]{2,1,0:T(8,128)(2,1)S(1)}, bf16[2,128,128]{2,1,0:T(8,128)(2,1)S(1)}, u32[]{:S(2)}, u32[]{:S(2)}) collective-permute-start(bf16[2,128,128]{2,1,0:T(8,128)(2,1)S(1)} %get-tuple-element.18), channel_id=1, source_target_pairs={{0,64},{64,0},{128,192},{192,128},{1,65},{65,1},{129,193},{193,129... | collective-permute-start | bytes 196616 | tf_op jit(solution)/shard_map/ppermute | solution.py:249
  3.0 2.8 %collective-permute-start.5 = (bf16[2,128,128]{2,1,0:T(8,128)(2,1)S(1)}, bf16[2,128,128]{2,1,0:T(8,128)(2,1)S(1)}, u32[]{:S(2)}, u32[]{:S(2)}) collective-permute-start(bf16[2,128,128]{2,1,0:T(8,128)(2,1)S(1)} %get-tuple-element.19), channel_id=1, source_target_pairs={{0,192},{64,128},{128,64},{192,0},{1,193},{65,129},{129,65},{193,1... | collective-permute-start | bytes 196616 | tf_op jit(solution)/shard_map/ppermute | solution.py:249
  5.8 0.5 collective-permute-start.4
  6.3 0.7 %broadcast_in_dim.32 = bf16[4,2,64,128]{3,2,1,0:T(8,128)(2,1)} broadcast(bf16[4,64,128]{2,1,0:T(8,128)(2,1)S(1)} %bitcast.17), dimensions={0,2,3} | broadcast | bytes 196608 | tf_op jit(solution)/shard_map/broadcast_in_dim | solution.py:243
  6.9 7.2 %all-to-all-start = ((bf16[8,64,128]{2,1,0:T(8,128)(2,1)}), bf16[8,64,128]{2,1,0:T(8,128)(2,1)S(1)}, u32[]{:S(2)}, u32[]{:S(2)}) async-start(bf16[8,64,128]{2,1,0:T(8,128)(2,1)} %bitcast.9), calls=%async_computation | async-start | bytes 262144 | tf_op jit(solution)/shard_map/all_to_all | solution.py:244
  14.3 1.7 %collective-permute-start.8 = (bf16[4,2,128,128]{3,2,1,0:T(8,128)(2,1)S(1)}, bf16[4,2,128,128]{3,2,1,0:T(8,128)(2,1)S(1)}, u32[]{:S(2)}, u32[]{:S(2)}) collective-permute-start(bf16[4,2,128,128]{3,2,1,0:T(8,128)(2,1)S(1)} %pad_maximum_fusion.a0), channel_id=1, source_target_pairs={{6,0},{0,2},{2,4},{4,6},{7,1},{1,3},{3,5},{5,7},{14,8},{8,10},{10,... | collective-permute-start | bytes 786440 | tf_op jit(solution)/shard_map/ppermute | solution.py:251
  15.9 2.9 %collective-permute-start.7 = (bf16[4,2,128,128]{3,2,1,0:T(8,128)(2,1)S(1)}, bf16[4,2,128,128]{3,2,1,0:T(8,128)(2,1)S(1)}, u32[]{:S(2)}, u32[]{:S(2)}) collective-permute-start(bf16[4,2,128,128]{3,2,1,0:T(8,128)(2,1)S(1)} %pad_maximum_fusion.a0), channel_id=1, source_target_pairs={{4,0},{6,2},{0,4},{2,6},{5,1},{7,3},{1,5},{3,7},{12,8},{14,10},{8,... | collective-permute-start | bytes 786440 | tf_op jit(solution)/shard_map/ppermute | solution.py:251
  18.8 1.3 %collective-permute-start.6 = (bf16[4,2,128,128]{3,2,1,0:T(8,128)(2,1)S(1)}, bf16[4,2,128,128]{3,2,1,0:T(8,128)(2,1)S(1)}, u32[]{:S(2)}, u32[]{:S(2)}) collective-permute-start(bf16[4,2,128,128]{3,2,1,0:T(8,128)(2,1)S(1)} %pad_maximum_fusion.a0), channel_id=1, source_target_pairs={{2,0},{4,2},{6,4},{0,6},{3,1},{5,3},{7,5},{1,7},{10,8},{12,10},{14... | collective-permute-start | bytes 786440 | tf_op jit(solution)/shard_map/ppermute | solution.py:251
  20.2 1.9 %all-to-all-done.q0 = bf16[8,64,128]{2,1,0:T(8,128)(2,1)S(1)} async-done(((bf16[8,64,128]{2,1,0:T(8,128)(2,1)}), bf16[8,64,128]{2,1,0:T(8,128)(2,1)S(1)}, u32[]{:S(2)}, u32[]{:S(2)}) %all-to-all-start) | async-done | bytes 131104 | tf_op jit(solution)/shard_map/all_to_all | solution.py:244
  22.0 1.5 %collective-permute-start.2 = (bf16[8,64,128]{2,1,0:T(8,128)(2,1)S(1)}, bf16[8,64,128]{2,1,0:T(8,128)(2,1)S(1)}, u32[]{:S(2)}, u32[]{:S(2)}) collective-permute-start(bf16[8,64,128]{2,1,0:T(8,128)(2,1)S(1)} %all-to-all-done.q0), channel_id=1, source_target_pairs={{48,0},{0,16},{16,32},{32,48},{49,1},{1,17},{17,33},{33,49},{50,2}... | collective-permute-start | bytes 393224 | tf_op jit(solution)/shard_map/ppermute | solution.py:245
  23.5 1.1 %collective-permute-start.1 = (bf16[8,64,128]{2,1,0:T(8,128)(2,1)S(1)}, bf16[8,64,128]{2,1,0:T(8,128)(2,1)S(1)}, u32[]{:S(2)}, u32[]{:S(2)}) collective-permute-start(bf16[8,64,128]{2,1,0:T(8,128)(2,1)S(1)} %all-to-all-done.q0), channel_id=1, source_target_pairs={{32,0},{48,16},{0,32},{16,48},{33,1},{49,17},{1,33},{17,49},{34,2}... | collective-permute-start | bytes 393224 | tf_op jit(solution)/shard_map/ppermute | solution.py:245
  24.6 0.2 select_reduce_fusion
  24.8 0.2 convert_reduce_fusion
  25.0 2.2 %collective-permute-start = (bf16[8,64,128]{2,1,0:T(8,128)(2,1)S(1)}, bf16[8,64,128]{2,1,0:T(8,128)(2,1)S(1)}, u32[]{:S(2)}, u32[]{:S(2)}) collective-permute-start(bf16[8,64,128]{2,1,0:T(8,128)(2,1)S(1)} %all-to-all-done.q0), channel_id=1, source_target_pairs={{16,0},{32,16},{48,32},{0,48},{17,1},{33,17},{49,33},{1,49},{18,2}... | collective-permute-start | bytes 393224 | tf_op jit(solution)/shard_map/ppermute | solution.py:245
  27.2 2.1 %collective-permute-done.7.a2 = bf16[4,2,128,128]{3,2,1,0:T(8,128)(2,1)S(1)} collective-permute-done((bf16[4,2,128,128]{3,2,1,0:T(8,128)(2,1)S(1)}, bf16[4,2,128,128]{3,2,1,0:T(8,128)(2,1)S(1)}, u32[]{:S(2)}, u32[]{:S(2)}) %collective-permute-start.7) | collective-permute-done | bytes 262176 | tf_op jit(solution)/shard_map/ppermute | solution.py:251
  29.3 0.5 collective-permute-start.12
  29.9 0.2 collective-permute-done.1.q2
  30.1 0.3 collective-permute-start.10
  30.5 0.9 %collective-permute-done.q1 = bf16[8,64,128]{2,1,0:T(8,128)(2,1)S(1)} collective-permute-done((bf16[8,64,128]{2,1,0:T(8,128)(2,1)S(1)}, bf16[8,64,128]{2,1,0:T(8,128)(2,1)S(1)}, u32[]{:S(2)}, u32[]{:S(2)}) %collective-permute-start) | collective-permute-done | bytes 131104 | tf_op jit(solution)/shard_map/ppermute | solution.py:245
  31.4 0.2 collective-permute-done.11.b2
  31.6 0.4 collective-permute-done.10.b1
  32.0 7.0 %attend.1 = (bf16[8,72,128]{2,1,0:T(8,128)(2,1)S(1)}, bf16[8,72,128]{2,1,0:T(8,128)(2,1)S(1)}, bf16[8,72,128]{2,1,0:T(8,128)(2,1)S(1)}, bf16[8,72,128]{2,1,0:T(8,128)(2,1)S(1)}) custom-call(s32[30]{0:T(128)S(1)} %concatenate.3.scal, bf16[8,64,128]{2,1,0:T(8,128)(2,1)S(1)} %all-to-all-done.q0, bf16[8,64,128]{2,1,0:T(8,128)(2,1)S(1)} %collective-permute-done.q1, ...), custom_call_target="tpu_custom_call" | custom-call | tf_op jit(solution)/shard_map/attend/pallas_call | solution.py:162
  39.0 1.6 %collective-permute-start.13 = (bf16[8,72,128]{2,1,0:T(8,128)(2,1)S(1)}, bf16[8,72,128]{2,1,0:T(8,128)(2,1)S(1)}, u32[]{:S(2)}, u32[]{:S(2)}) collective-permute-start(bf16[8,72,128]{2,1,0:T(8,128)(2,1)S(1)} %get-tuple-element.14), channel_id=1, source_target_pairs={{48,0},{0,16},{16,32},{32,48},{49,1},{1,17},{17,33},{33,49},{50,2}... | collective-permute-start | bytes 442376 | tf_op jit(solution)/shard_map/ppermute | solution.py:266
  40.5 1.3 %collective-permute-start.14 = (bf16[8,72,128]{2,1,0:T(8,128)(2,1)S(1)}, bf16[8,72,128]{2,1,0:T(8,128)(2,1)S(1)}, u32[]{:S(2)}, u32[]{:S(2)}) collective-permute-start(bf16[8,72,128]{2,1,0:T(8,128)(2,1)S(1)} %get-tuple-element.15), channel_id=1, source_target_pairs={{32,0},{48,16},{0,32},{16,48},{33,1},{49,17},{1,33},{17,49},{34,2}... | collective-permute-start | bytes 442376 | tf_op jit(solution)/shard_map/ppermute | solution.py:266
  41.8 2.0 %collective-permute-start.15 = (bf16[8,72,128]{2,1,0:T(8,128)(2,1)S(1)}, bf16[8,72,128]{2,1,0:T(8,128)(2,1)S(1)}, u32[]{:S(2)}, u32[]{:S(2)}) collective-permute-start(bf16[8,72,128]{2,1,0:T(8,128)(2,1)S(1)} %get-tuple-element.16), channel_id=1, source_target_pairs={{16,0},{32,16},{48,32},{0,48},{17,1},{33,17},{49,33},{1,49},{18,2}... | collective-permute-start | bytes 442376 | tf_op jit(solution)/shard_map/ppermute | solution.py:266
  43.8 1.8 %collective-permute-done.13.p1 = bf16[8,72,128]{2,1,0:T(8,128)(2,1)S(1)} collective-permute-done((bf16[8,72,128]{2,1,0:T(8,128)(2,1)S(1)}, bf16[8,72,128]{2,1,0:T(8,128)(2,1)S(1)}, u32[]{:S(2)}, u32[]{:S(2)}) %collective-permute-start.13) | collective-permute-done | bytes 147488 | tf_op jit(solution)/shard_map/ppermute | solution.py:266
  45.6 3.2 %collective-permute-done.14.p2 = bf16[8,72,128]{2,1,0:T(8,128)(2,1)S(1)} collective-permute-done((bf16[8,72,128]{2,1,0:T(8,128)(2,1)S(1)}, bf16[8,72,128]{2,1,0:T(8,128)(2,1)S(1)}, u32[]{:S(2)}, u32[]{:S(2)}) %collective-permute-start.14) | collective-permute-done | bytes 147488 | tf_op jit(solution)/shard_map/ppermute | solution.py:266
  48.7 1.5 %collective-permute-done.15.p3 = bf16[8,72,128]{2,1,0:T(8,128)(2,1)S(1)} collective-permute-done((bf16[8,72,128]{2,1,0:T(8,128)(2,1)S(1)}, bf16[8,72,128]{2,1,0:T(8,128)(2,1)S(1)}, u32[]{:S(2)}, u32[]{:S(2)}) %collective-permute-start.15) | collective-permute-done | bytes 147488 | tf_op jit(solution)/shard_map/ppermute | solution.py:266
  50.3 0.6 merge.1
  50.9 12.5 %all_to_all.10.parts = bf16[8,72,128]{2,1,0:T(8,128)(2,1)S(1)} all-to-all(bf16[8,72,128]{2,1,0:T(8,128)(2,1)S(1)} %merge.1), channel_id=1, replica_groups=mesh['zl'=4,'x'=4,'zh'=2,'y'=4,'core'=2] {'zl','zh'}, dimensions={0} | all-to-all | bytes 294912 | tf_op jit(solution)/shard_map/all_to_all | solution.py:275
  63.4 1.5 %combine.1 = bf16[4,8192]{1,0:T(4,128)(2,1)} custom-call(s32[30]{0:T(128)S(1)} %concatenate.3.scal, bf16[8,72,128]{2,1,0:T(8,128)(2,1)S(1)} %all_to_all.10.parts), custom_call_target="tpu_custom_call" | custom-call | tf_op jit(solution)/shard_map/combine/pallas_call | solution.py:276
  (19 shorter events, 0.3 us)
Async XLA Ops:
  0.0 6.3 %copy-start = (bf16[4,8192]{1,0:T(4,128)(2,1)S(1)}, bf16[4,8192]{1,0:T(4,128)(2,1)}, u32[]{:S(2)}) copy-start(bf16[4,8192]{1,0:T(4,128)(2,1)} %param.3) | copy-start | bytes 196612
  1.0 13.2 %collective-permute-start.3 = (bf16[2,128,128]{2,1,0:T(8,128)(2,1)S(1)}, bf16[2,128,128]{2,1,0:T(8,128)(2,1)S(1)}, u32[]{:S(2)}, u32[]{:S(2)}) collective-permute-start(bf16[2,128,128]{2,1,0:T(8,128)(2,1)S(1)} %get-tuple-element.18), channel_id=1, source_target_pairs={{0,64},{64,0},{128,192},{192,128},{1,65},{65,1},{129,193},{193,129... | collective-permute-start | bytes 196616 | tf_op jit(solution)/shard_map/ppermute | solution.py:249
  3.0 11.2 %collective-permute-start.5 = (bf16[2,128,128]{2,1,0:T(8,128)(2,1)S(1)}, bf16[2,128,128]{2,1,0:T(8,128)(2,1)S(1)}, u32[]{:S(2)}, u32[]{:S(2)}) collective-permute-start(bf16[2,128,128]{2,1,0:T(8,128)(2,1)S(1)} %get-tuple-element.19), channel_id=1, source_target_pairs={{0,192},{64,128},{128,64},{192,0},{1,193},{65,129},{129,65},{193,1... | collective-permute-start | bytes 196616 | tf_op jit(solution)/shard_map/ppermute | solution.py:249
  5.8 8.4 %collective-permute-start.4 = (bf16[2,128,128]{2,1,0:T(8,128)(2,1)S(1)}, bf16[2,128,128]{2,1,0:T(8,128)(2,1)S(1)}, u32[]{:S(2)}, u32[]{:S(2)}) collective-permute-start(bf16[2,128,128]{2,1,0:T(8,128)(2,1)S(1)} %get-tuple-element.20), channel_id=1, source_target_pairs={{0,128},{64,192},{128,0},{192,64},{1,129},{65,193},{129,1},{193,65... | collective-permute-start | bytes 196616 | tf_op jit(solution)/shard_map/ppermute | solution.py:249
  6.9 15.1 %all-to-all-start = ((bf16[8,64,128]{2,1,0:T(8,128)(2,1)}), bf16[8,64,128]{2,1,0:T(8,128)(2,1)S(1)}, u32[]{:S(2)}, u32[]{:S(2)}) async-start(bf16[8,64,128]{2,1,0:T(8,128)(2,1)} %bitcast.9), calls=%async_computation | async-start | bytes 262144 | tf_op jit(solution)/shard_map/all_to_all | solution.py:244
  14.2 10.4 %copy-start.1 = (s32[256]{0:T(256)S(1)}, s32[256]{0:T(256)}, u32[]{:S(2)}) copy-start(s32[256]{0:T(256)} %param.5) | copy-start | bytes 3076
  14.3 10.8 %collective-permute-start.8 = (bf16[4,2,128,128]{3,2,1,0:T(8,128)(2,1)S(1)}, bf16[4,2,128,128]{3,2,1,0:T(8,128)(2,1)S(1)}, u32[]{:S(2)}, u32[]{:S(2)}) collective-permute-start(bf16[4,2,128,128]{3,2,1,0:T(8,128)(2,1)S(1)} %pad_maximum_fusion.a0), channel_id=1, source_target_pairs={{6,0},{0,2},{2,4},{4,6},{7,1},{1,3},{3,5},{5,7},{14,8},{8,10},{10,... | collective-permute-start | bytes 786440 | tf_op jit(solution)/shard_map/ppermute | solution.py:251
  15.9 13.4 %collective-permute-start.7 = (bf16[4,2,128,128]{3,2,1,0:T(8,128)(2,1)S(1)}, bf16[4,2,128,128]{3,2,1,0:T(8,128)(2,1)S(1)}, u32[]{:S(2)}, u32[]{:S(2)}) collective-permute-start(bf16[4,2,128,128]{3,2,1,0:T(8,128)(2,1)S(1)} %pad_maximum_fusion.a0), channel_id=1, source_target_pairs={{4,0},{6,2},{0,4},{2,6},{5,1},{7,3},{1,5},{3,7},{12,8},{14,10},{8,... | collective-permute-start | bytes 786440 | tf_op jit(solution)/shard_map/ppermute | solution.py:251
  18.8 10.5 %collective-permute-start.6 = (bf16[4,2,128,128]{3,2,1,0:T(8,128)(2,1)S(1)}, bf16[4,2,128,128]{3,2,1,0:T(8,128)(2,1)S(1)}, u32[]{:S(2)}, u32[]{:S(2)}) collective-permute-start(bf16[4,2,128,128]{3,2,1,0:T(8,128)(2,1)S(1)} %pad_maximum_fusion.a0), channel_id=1, source_target_pairs={{2,0},{4,2},{6,4},{0,6},{3,1},{5,3},{7,5},{1,7},{10,8},{12,10},{14... | collective-permute-start | bytes 786440 | tf_op jit(solution)/shard_map/ppermute | solution.py:251
  22.0 7.8 %collective-permute-start.2 = (bf16[8,64,128]{2,1,0:T(8,128)(2,1)S(1)}, bf16[8,64,128]{2,1,0:T(8,128)(2,1)S(1)}, u32[]{:S(2)}, u32[]{:S(2)}) collective-permute-start(bf16[8,64,128]{2,1,0:T(8,128)(2,1)S(1)} %all-to-all-done.q0), channel_id=1, source_target_pairs={{48,0},{0,16},{16,32},{32,48},{49,1},{1,17},{17,33},{33,49},{50,2}... | collective-permute-start | bytes 393224 | tf_op jit(solution)/shard_map/ppermute | solution.py:245
  23.5 6.6 %collective-permute-start.1 = (bf16[8,64,128]{2,1,0:T(8,128)(2,1)S(1)}, bf16[8,64,128]{2,1,0:T(8,128)(2,1)S(1)}, u32[]{:S(2)}, u32[]{:S(2)}) collective-permute-start(bf16[8,64,128]{2,1,0:T(8,128)(2,1)S(1)} %all-to-all-done.q0), channel_id=1, source_target_pairs={{32,0},{48,16},{0,32},{16,48},{33,1},{49,17},{1,33},{17,49},{34,2}... | collective-permute-start | bytes 393224 | tf_op jit(solution)/shard_map/ppermute | solution.py:245
  25.0 6.4 %collective-permute-start = (bf16[8,64,128]{2,1,0:T(8,128)(2,1)S(1)}, bf16[8,64,128]{2,1,0:T(8,128)(2,1)S(1)}, u32[]{:S(2)}, u32[]{:S(2)}) collective-permute-start(bf16[8,64,128]{2,1,0:T(8,128)(2,1)S(1)} %all-to-all-done.q0), channel_id=1, source_target_pairs={{16,0},{32,16},{48,32},{0,48},{17,1},{33,17},{49,33},{1,49},{18,2}... | collective-permute-start | bytes 393224 | tf_op jit(solution)/shard_map/ppermute | solution.py:245
  29.3 2.1 %collective-permute-start.9 = (bf16[4,2,128,128]{3,2,1,0:T(8,128)(2,1)S(1)}, bf16[4,2,128,128]{3,2,1,0:T(8,128)(2,1)S(1)}, u32[]{:S(2)}, u32[]{:S(2)}) collective-permute-start(bf16[4,2,128,128]{3,2,1,0:T(8,128)(2,1)S(1)} %pad_maximum_fusion.a0), channel_id=1, source_target_pairs={{0,1},{1,0},{2,3},{3,2},{4,5},{5,4},{6,7},{7,6},{8,9},{9,8},{10,11... | collective-permute-start | bytes 786440 | tf_op jit(solution)/shard_map/ppermute | solution.py:254
  29.3 2.1 %collective-permute-start.12 = (bf16[4,2,128,128]{3,2,1,0:T(8,128)(2,1)S(1)}, bf16[4,2,128,128]{3,2,1,0:T(8,128)(2,1)S(1)}, u32[]{:S(2)}, u32[]{:S(2)}) collective-permute-start(bf16[4,2,128,128]{3,2,1,0:T(8,128)(2,1)S(1)} %collective-permute-done.8.a3), channel_id=1, source_target_pairs={{0,1},{1,0},{2,3},{3,2},{4,5},{5,4},{6,7},{7,6},{8,9},{9,8},{10,11... | collective-permute-start | bytes 786440 | tf_op jit(solution)/shard_map/ppermute | solution.py:254
  29.8 1.8 %collective-permute-start.11 = (bf16[4,2,128,128]{3,2,1,0:T(8,128)(2,1)S(1)}, bf16[4,2,128,128]{3,2,1,0:T(8,128)(2,1)S(1)}, u32[]{:S(2)}, u32[]{:S(2)}) collective-permute-start(bf16[4,2,128,128]{3,2,1,0:T(8,128)(2,1)S(1)} %collective-permute-done.7.a2), channel_id=1, source_target_pairs={{0,1},{1,0},{2,3},{3,2},{4,5},{5,4},{6,7},{7,6},{8,9},{9,8},{10,11... | collective-permute-start | bytes 786440 | tf_op jit(solution)/shard_map/ppermute | solution.py:254
  30.1 1.9 %collective-permute-start.10 = (bf16[4,2,128,128]{3,2,1,0:T(8,128)(2,1)S(1)}, bf16[4,2,128,128]{3,2,1,0:T(8,128)(2,1)S(1)}, u32[]{:S(2)}, u32[]{:S(2)}) collective-permute-start(bf16[4,2,128,128]{3,2,1,0:T(8,128)(2,1)S(1)} %collective-permute-done.6.a1), channel_id=1, source_target_pairs={{0,1},{1,0},{2,3},{3,2},{4,5},{5,4},{6,7},{7,6},{8,9},{9,8},{10,11... | collective-permute-start | bytes 786440 | tf_op jit(solution)/shard_map/ppermute | solution.py:254
  39.0 6.6 %collective-permute-start.13 = (bf16[8,72,128]{2,1,0:T(8,128)(2,1)S(1)}, bf16[8,72,128]{2,1,0:T(8,128)(2,1)S(1)}, u32[]{:S(2)}, u32[]{:S(2)}) collective-permute-start(bf16[8,72,128]{2,1,0:T(8,128)(2,1)S(1)} %get-tuple-element.14), channel_id=1, source_target_pairs={{48,0},{0,16},{16,32},{32,48},{49,1},{1,17},{17,33},{33,49},{50,2}... | collective-permute-start | bytes 442376 | tf_op jit(solution)/shard_map/ppermute | solution.py:266
  40.5 8.2 %collective-permute-start.14 = (bf16[8,72,128]{2,1,0:T(8,128)(2,1)S(1)}, bf16[8,72,128]{2,1,0:T(8,128)(2,1)S(1)}, u32[]{:S(2)}, u32[]{:S(2)}) collective-permute-start(bf16[8,72,128]{2,1,0:T(8,128)(2,1)S(1)} %get-tuple-element.15), channel_id=1, source_target_pairs={{32,0},{48,16},{0,32},{16,48},{33,1},{49,17},{1,33},{17,49},{34,2}... | collective-permute-start | bytes 442376 | tf_op jit(solution)/shard_map/ppermute | solution.py:266
  41.8 8.5 %collective-permute-start.15 = (bf16[8,72,128]{2,1,0:T(8,128)(2,1)S(1)}, bf16[8,72,128]{2,1,0:T(8,128)(2,1)S(1)}, u32[]{:S(2)}, u32[]{:S(2)}) collective-permute-start(bf16[8,72,128]{2,1,0:T(8,128)(2,1)S(1)} %get-tuple-element.16), channel_id=1, source_target_pairs={{16,0},{32,16},{48,32},{0,48},{17,1},{33,17},{49,33},{1,49},{18,2}... | collective-permute-start | bytes 442376 | tf_op jit(solution)/shard_map/ppermute | solution.py:266

commit v3 on v2

--- a/solution.py
+++ b/solution.py
@@ -244,9 +244,12 @@
     q = lax.all_to_all(q, ("zl", "zh"), 0, 0, tiled=True)
     q = [q, *(lax.ppermute(q, "x", turned(k)) for k in (1, 2, 3))]
     pieces = []
-    for s in range(4):
-        piece = lax.dynamic_slice_in_dim(keys_values, (zl ^ s) * WIDTH, WIDTH, 2)
+    source = keys_values
+    for s in (1, 2, 3, 0):
+        piece = lax.dynamic_slice_in_dim(source, (zl ^ s) * WIDTH, WIDTH, 2)
+        piece, source = lax.optimization_barrier((piece, source))
         pieces.append(lax.ppermute(piece, "zl", [(i, i ^ s) for i in range(4)]) if s else piece)
+    pieces = [pieces[3], *pieces[:3]]
     a0 = jnp.stack(pieces)
     a1, a2, a3 = (lax.ppermute(a0, "y", turned(k)) for k in (1, 2, 3))
     swap = [(0, 1), (1, 0)]

time: 66.1 us -> 66.1 us (level)
  the two profiles are of different devices: /device:TPU:2 before, /device:TPU:32 now
where the time goes in v3:
time: 66.1 us; the launch traced here: 66.3 us
  starting transfers between devices  31 us (47%)
  blocking collectives  14.1 us (21%)
  waiting for transfers between devices  10.5 us (16%)
  Pallas kernels  8.32 us (13%)
  local copies, waits for them, and re-layouts  1.76 us (3%)
    all_to_all x1, blocking collectives, per_device(): part = lax.all_to_all(part, ('zl', 'zh'), 0, 0, tiled=True)  14.1 us
    all_to_all x1, starting transfers between devices, per_device(): q = lax.all_to_all(q, ('zl', 'zh'), 0, 0, tiled=True)  8.22 us
    pallas_call x1, Pallas kernels, attend_call(): pl.pallas_call(attend, out_shape=(jax.ShapeDtypeStruct((8, SLOT_ROWS, WID...  6.24 us
    ppermute x3, starting transfers between devices, per_device(): a1, a2, a3 = (lax.ppermute(a0, 'y', turned(k)) for k in (1, 2, 3))  5.9 us
    ppermute x3, waiting for transfers between devices, per_device(): lax.ppermute(part[k], 'x', turned(4 - k))  5.78 us
    ppermute x3, starting transfers between devices, per_device(): lax.ppermute(part[k], 'x', turned(4 - k))  5.74 us
    ppermute x3, starting transfers between devices, per_device(): q = [q, *(lax.ppermute(q, 'x', turned(k)) for k in (1, 2, 3))]  5.73 us
    ppermute x3, starting transfers between devices, per_device(): lax.ppermute(piece, 'zl', [(i, i ^ s) for i in range(4)])  4.82 us
  transfers between devices with their start and end apart: 17, of which 8 were waited for; matrix products, arithmetic and copies ran while one was open for 2% of the time, Pallas kernels for 0%

profile of v3, /device:TPU:32, one launch (start us, length us, event | category | flops | bytes accessed | tf_op | source)
XLA Modules:
  0.0 66.3 jit_solution(3294983735283843156)
XLA Ops:
  0.0 0.9 %copy-done = bf16[2,128,512]{2,1,0:T(8,128)(2,1)S(1)} copy-done((bf16[2,128,512]{2,1,0:T(8,128)(2,1)S(1)}, bf16[2,128,512]{2,1,0:T(8,128)(2,1)}, u32[]{:S(2)}) %copy-start) | copy-done | bytes 262168
  1.0 2.0 %collective-permute-start.5 = (bf16[2,128,128]{2,1,0:T(8,128)(2,1)S(1)}, bf16[2,128,128]{2,1,0:T(8,128)(2,1)S(1)}, u32[]{:S(2)}, u32[]{:S(2)}) collective-permute-start(bf16[2,128,128]{2,1,0:T(8,128)(2,1)S(1)} %constant_dynamic-slice_fusion), channel_id=1, source_target_pairs={{0,192},{64,128},{128,64},{192,0},{1,193},{65,129},{129,65},{193,1... | collective-permute-start | bytes 196616 | tf_op jit(solution)/shard_map/ppermute | solution.py:251
  3.0 2.3 %collective-permute-start.4 = (bf16[2,128,128]{2,1,0:T(8,128)(2,1)S(1)}, bf16[2,128,128]{2,1,0:T(8,128)(2,1)S(1)}, u32[]{:S(2)}, u32[]{:S(2)}) collective-permute-start(bf16[2,128,128]{2,1,0:T(8,128)(2,1)S(1)} %constant_dynamic-slice_fusion.1), channel_id=1, source_target_pairs={{0,128},{64,192},{128,0},{192,64},{1,129},{65,193},{129,1},{193,65... | collective-permute-start | bytes 196616 | tf_op jit(solution)/shard_map/ppermute | solution.py:251
  5.3 0.5 collective-permute-start.3
  5.9 0.7 %broadcast_in_dim.32 = bf16[4,2,64,128]{3,2,1,0:T(8,128)(2,1)} broadcast(bf16[4,64,128]{2,1,0:T(8,128)(2,1)S(1)} %bitcast.17), dimensions={0,2,3} | broadcast | bytes 196608 | tf_op jit(solution)/shard_map/broadcast_in_dim | solution.py:243
  6.5 8.2 %all-to-all-start = ((bf16[8,64,128]{2,1,0:T(8,128)(2,1)}), bf16[8,64,128]{2,1,0:T(8,128)(2,1)S(1)}, u32[]{:S(2)}, u32[]{:S(2)}) async-start(bf16[8,64,128]{2,1,0:T(8,128)(2,1)} %bitcast.9), calls=%async_computation | async-start | bytes 262144 | tf_op jit(solution)/shard_map/all_to_all | solution.py:244
  14.9 1.7 %collective-permute-start.8 = (bf16[4,2,128,128]{3,2,1,0:T(8,128)(2,1)S(1)}, bf16[4,2,128,128]{3,2,1,0:T(8,128)(2,1)S(1)}, u32[]{:S(2)}, u32[]{:S(2)}) collective-permute-start(bf16[4,2,128,128]{3,2,1,0:T(8,128)(2,1)S(1)} %pad_maximum_fusion.a0), channel_id=1, source_target_pairs={{6,0},{0,2},{2,4},{4,6},{7,1},{1,3},{3,5},{5,7},{14,8},{8,10},{10,... | collective-permute-start | bytes 786440 | tf_op jit(solution)/shard_map/ppermute | solution.py:254
  16.5 2.9 %collective-permute-start.7 = (bf16[4,2,128,128]{3,2,1,0:T(8,128)(2,1)S(1)}, bf16[4,2,128,128]{3,2,1,0:T(8,128)(2,1)S(1)}, u32[]{:S(2)}, u32[]{:S(2)}) collective-permute-start(bf16[4,2,128,128]{3,2,1,0:T(8,128)(2,1)S(1)} %pad_maximum_fusion.a0), channel_id=1, source_target_pairs={{4,0},{6,2},{0,4},{2,6},{5,1},{7,3},{1,5},{3,7},{12,8},{14,10},{8,... | collective-permute-start | bytes 786440 | tf_op jit(solution)/shard_map/ppermute | solution.py:254
  19.4 1.3 %collective-permute-start.6 = (bf16[4,2,128,128]{3,2,1,0:T(8,128)(2,1)S(1)}, bf16[4,2,128,128]{3,2,1,0:T(8,128)(2,1)S(1)}, u32[]{:S(2)}, u32[]{:S(2)}) collective-permute-start(bf16[4,2,128,128]{3,2,1,0:T(8,128)(2,1)S(1)} %pad_maximum_fusion.a0), channel_id=1, source_target_pairs={{2,0},{4,2},{6,4},{0,6},{3,1},{5,3},{7,5},{1,7},{10,8},{12,10},{14... | collective-permute-start | bytes 786440 | tf_op jit(solution)/shard_map/ppermute | solution.py:254
  20.8 1.4 %all-to-all-done.q0 = bf16[8,64,128]{2,1,0:T(8,128)(2,1)S(1)} async-done(((bf16[8,64,128]{2,1,0:T(8,128)(2,1)}), bf16[8,64,128]{2,1,0:T(8,128)(2,1)S(1)}, u32[]{:S(2)}, u32[]{:S(2)}) %all-to-all-start) | async-done | bytes 131104 | tf_op jit(solution)/shard_map/all_to_all | solution.py:244
  22.2 1.5 %collective-permute-start.2 = (bf16[8,64,128]{2,1,0:T(8,128)(2,1)S(1)}, bf16[8,64,128]{2,1,0:T(8,128)(2,1)S(1)}, u32[]{:S(2)}, u32[]{:S(2)}) collective-permute-start(bf16[8,64,128]{2,1,0:T(8,128)(2,1)S(1)} %all-to-all-done.q0), channel_id=1, source_target_pairs={{48,0},{0,16},{16,32},{32,48},{49,1},{1,17},{17,33},{33,49},{50,2}... | collective-permute-start | bytes 393224 | tf_op jit(solution)/shard_map/ppermute | solution.py:245
  23.7 2.7 %collective-permute-start.1 = (bf16[8,64,128]{2,1,0:T(8,128)(2,1)S(1)}, bf16[8,64,128]{2,1,0:T(8,128)(2,1)S(1)}, u32[]{:S(2)}, u32[]{:S(2)}) collective-permute-start(bf16[8,64,128]{2,1,0:T(8,128)(2,1)S(1)} %all-to-all-done.q0), channel_id=1, source_target_pairs={{32,0},{48,16},{0,32},{16,48},{33,1},{49,17},{1,33},{17,49},{34,2}... | collective-permute-start | bytes 393224 | tf_op jit(solution)/shard_map/ppermute | solution.py:245
  26.4 0.2 select_reduce_fusion
  26.6 0.2 convert_reduce_fusion
  26.8 1.5 %collective-permute-start = (bf16[8,64,128]{2,1,0:T(8,128)(2,1)S(1)}, bf16[8,64,128]{2,1,0:T(8,128)(2,1)S(1)}, u32[]{:S(2)}, u32[]{:S(2)}) collective-permute-start(bf16[8,64,128]{2,1,0:T(8,128)(2,1)S(1)} %all-to-all-done.q0), channel_id=1, source_target_pairs={{16,0},{32,16},{48,32},{0,48},{17,1},{33,17},{49,33},{1,49},{18,2}... | collective-permute-start | bytes 393224 | tf_op jit(solution)/shard_map/ppermute | solution.py:245
  28.3 1.3 %collective-permute-done.7.a2 = bf16[4,2,128,128]{3,2,1,0:T(8,128)(2,1)S(1)} collective-permute-done((bf16[4,2,128,128]{3,2,1,0:T(8,128)(2,1)S(1)}, bf16[4,2,128,128]{3,2,1,0:T(8,128)(2,1)S(1)}, u32[]{:S(2)}, u32[]{:S(2)}) %collective-permute-start.7) | collective-permute-done | bytes 262176 | tf_op jit(solution)/shard_map/ppermute | solution.py:254
  29.7 0.5 collective-permute-start.12
  30.2 0.1 collective-permute-start.11
  30.3 0.5 collective-permute-done.1.q2
  30.8 0.1 concatenate.3.scal
  30.9 1.0 %collective-permute-done.q1 = bf16[8,64,128]{2,1,0:T(8,128)(2,1)S(1)} collective-permute-done((bf16[8,64,128]{2,1,0:T(8,128)(2,1)S(1)}, bf16[8,64,128]{2,1,0:T(8,128)(2,1)S(1)}, u32[]{:S(2)}, u32[]{:S(2)}) %collective-permute-start) | collective-permute-done | bytes 131104 | tf_op jit(solution)/shard_map/ppermute | solution.py:245
  31.8 0.1 collective-permute-done.11.b2
  31.9 0.4 collective-permute-done.10.b1
  32.3 6.2 %attend.1 = (bf16[8,72,128]{2,1,0:T(8,128)(2,1)S(1)}, bf16[8,72,128]{2,1,0:T(8,128)(2,1)S(1)}, bf16[8,72,128]{2,1,0:T(8,128)(2,1)S(1)}, bf16[8,72,128]{2,1,0:T(8,128)(2,1)S(1)}) custom-call(s32[30]{0:T(128)S(1)} %concatenate.3.scal, bf16[8,64,128]{2,1,0:T(8,128)(2,1)S(1)} %all-to-all-done.q0, bf16[8,64,128]{2,1,0:T(8,128)(2,1)S(1)} %collective-permute-done.q1, ...), custom_call_target="tpu_custom_call" | custom-call | tf_op jit(solution)/shard_map/attend/pallas_call | solution.py:162
  38.6 1.6 %collective-permute-start.13 = (bf16[8,72,128]{2,1,0:T(8,128)(2,1)S(1)}, bf16[8,72,128]{2,1,0:T(8,128)(2,1)S(1)}, u32[]{:S(2)}, u32[]{:S(2)}) collective-permute-start(bf16[8,72,128]{2,1,0:T(8,128)(2,1)S(1)} %get-tuple-element.28), channel_id=1, source_target_pairs={{48,0},{0,16},{16,32},{32,48},{49,1},{1,17},{17,33},{33,49},{50,2}... | collective-permute-start | bytes 442376 | tf_op jit(solution)/shard_map/ppermute | solution.py:269
  40.1 2.9 %collective-permute-start.14 = (bf16[8,72,128]{2,1,0:T(8,128)(2,1)S(1)}, bf16[8,72,128]{2,1,0:T(8,128)(2,1)S(1)}, u32[]{:S(2)}, u32[]{:S(2)}) collective-permute-start(bf16[8,72,128]{2,1,0:T(8,128)(2,1)S(1)} %get-tuple-element.29), channel_id=1, source_target_pairs={{32,0},{48,16},{0,32},{16,48},{33,1},{49,17},{1,33},{17,49},{34,2}... | collective-permute-start | bytes 442376 | tf_op jit(solution)/shard_map/ppermute | solution.py:269
  43.0 1.3 %collective-permute-start.15 = (bf16[8,72,128]{2,1,0:T(8,128)(2,1)S(1)}, bf16[8,72,128]{2,1,0:T(8,128)(2,1)S(1)}, u32[]{:S(2)}, u32[]{:S(2)}) collective-permute-start(bf16[8,72,128]{2,1,0:T(8,128)(2,1)S(1)} %get-tuple-element.30), channel_id=1, source_target_pairs={{16,0},{32,16},{48,32},{0,48},{17,1},{33,17},{49,33},{1,49},{18,2}... | collective-permute-start | bytes 442376 | tf_op jit(solution)/shard_map/ppermute | solution.py:269
  44.3 1.4 %collective-permute-done.13.p1 = bf16[8,72,128]{2,1,0:T(8,128)(2,1)S(1)} collective-permute-done((bf16[8,72,128]{2,1,0:T(8,128)(2,1)S(1)}, bf16[8,72,128]{2,1,0:T(8,128)(2,1)S(1)}, u32[]{:S(2)}, u32[]{:S(2)}) %collective-permute-start.13) | collective-permute-done | bytes 147488 | tf_op jit(solution)/shard_map/ppermute | solution.py:269
  45.7 4.3 %collective-permute-done.14.p2 = bf16[8,72,128]{2,1,0:T(8,128)(2,1)S(1)} collective-permute-done((bf16[8,72,128]{2,1,0:T(8,128)(2,1)S(1)}, bf16[8,72,128]{2,1,0:T(8,128)(2,1)S(1)}, u32[]{:S(2)}, u32[]{:S(2)}) %collective-permute-start.14) | collective-permute-done | bytes 147488 | tf_op jit(solution)/shard_map/ppermute | solution.py:269
  50.1 0.6 merge.1
  50.7 14.1 %all_to_all.10.parts = bf16[8,72,128]{2,1,0:T(8,128)(2,1)S(1)} all-to-all(bf16[8,72,128]{2,1,0:T(8,128)(2,1)S(1)} %merge.1), channel_id=1, replica_groups=mesh['zl'=4,'x'=4,'zh'=2,'y'=4,'core'=2] {'zl','zh'}, dimensions={0} | all-to-all | bytes 294912 | tf_op jit(solution)/shard_map/all_to_all | solution.py:278
  64.8 1.5 %combine.1 = bf16[4,8192]{1,0:T(4,128)(2,1)} custom-call(s32[30]{0:T(128)S(1)} %concatenate.3.scal, bf16[8,72,128]{2,1,0:T(8,128)(2,1)S(1)} %all_to_all.10.parts), custom_call_target="tpu_custom_call" | custom-call | tf_op jit(solution)/shard_map/combine/pallas_call | solution.py:279
  (24 shorter events, 0.2 us)
Async XLA Ops:
  0.0 1.0 %copy-start = (bf16[2,128,512]{2,1,0:T(8,128)(2,1)S(1)}, bf16[2,128,512]{2,1,0:T(8,128)(2,1)}, u32[]{:S(2)}) copy-start(bf16[2,128,512]{2,1,0:T(8,128)(2,1)} %param.4) | copy-start | bytes 786436
  1.0 4.9 %copy-start.1 = (bf16[4,8192]{1,0:T(4,128)(2,1)S(1)}, bf16[4,8192]{1,0:T(4,128)(2,1)}, u32[]{:S(2)}) copy-start(bf16[4,8192]{1,0:T(4,128)(2,1)} %param.3) | copy-start | bytes 196612
  1.0 13.7 %collective-permute-start.5 = (bf16[2,128,128]{2,1,0:T(8,128)(2,1)S(1)}, bf16[2,128,128]{2,1,0:T(8,128)(2,1)S(1)}, u32[]{:S(2)}, u32[]{:S(2)}) collective-permute-start(bf16[2,128,128]{2,1,0:T(8,128)(2,1)S(1)} %constant_dynamic-slice_fusion), channel_id=1, source_target_pairs={{0,192},{64,128},{128,64},{192,0},{1,193},{65,129},{129,65},{193,1... | collective-permute-start | bytes 196616 | tf_op jit(solution)/shard_map/ppermute | solution.py:251
  3.0 11.7 %collective-permute-start.4 = (bf16[2,128,128]{2,1,0:T(8,128)(2,1)S(1)}, bf16[2,128,128]{2,1,0:T(8,128)(2,1)S(1)}, u32[]{:S(2)}, u32[]{:S(2)}) collective-permute-start(bf16[2,128,128]{2,1,0:T(8,128)(2,1)S(1)} %constant_dynamic-slice_fusion.1), channel_id=1, source_target_pairs={{0,128},{64,192},{128,0},{192,64},{1,129},{65,193},{129,1},{193,65... | collective-permute-start | bytes 196616 | tf_op jit(solution)/shard_map/ppermute | solution.py:251
  5.3 9.5 %collective-permute-start.3 = (bf16[2,128,128]{2,1,0:T(8,128)(2,1)S(1)}, bf16[2,128,128]{2,1,0:T(8,128)(2,1)S(1)}, u32[]{:S(2)}, u32[]{:S(2)}) collective-permute-start(bf16[2,128,128]{2,1,0:T(8,128)(2,1)S(1)} %constant_dynamic-slice_fusion.2), channel_id=1, source_target_pairs={{0,64},{64,0},{128,192},{192,128},{1,65},{65,1},{129,193},{193,129... | collective-permute-start | bytes 196616 | tf_op jit(solution)/shard_map/ppermute | solution.py:251
  6.5 15.7 %all-to-all-start = ((bf16[8,64,128]{2,1,0:T(8,128)(2,1)}), bf16[8,64,128]{2,1,0:T(8,128)(2,1)S(1)}, u32[]{:S(2)}, u32[]{:S(2)}) async-start(bf16[8,64,128]{2,1,0:T(8,128)(2,1)} %bitcast.9), calls=%async_computation | async-start | bytes 262144 | tf_op jit(solution)/shard_map/all_to_all | solution.py:244
  14.8 11.6 %copy-start.2 = (s32[256]{0:T(256)S(1)}, s32[256]{0:T(256)}, u32[]{:S(2)}) copy-start(s32[256]{0:T(256)} %param.5) | copy-start | bytes 3076
  14.9 11.9 %collective-permute-start.8 = (bf16[4,2,128,128]{3,2,1,0:T(8,128)(2,1)S(1)}, bf16[4,2,128,128]{3,2,1,0:T(8,128)(2,1)S(1)}, u32[]{:S(2)}, u32[]{:S(2)}) collective-permute-start(bf16[4,2,128,128]{3,2,1,0:T(8,128)(2,1)S(1)} %pad_maximum_fusion.a0), channel_id=1, source_target_pairs={{6,0},{0,2},{2,4},{4,6},{7,1},{1,3},{3,5},{5,7},{14,8},{8,10},{10,... | collective-permute-start | bytes 786440 | tf_op jit(solution)/shard_map/ppermute | solution.py:254
  16.5 13.1 %collective-permute-start.7 = (bf16[4,2,128,128]{3,2,1,0:T(8,128)(2,1)S(1)}, bf16[4,2,128,128]{3,2,1,0:T(8,128)(2,1)S(1)}, u32[]{:S(2)}, u32[]{:S(2)}) collective-permute-start(bf16[4,2,128,128]{3,2,1,0:T(8,128)(2,1)S(1)} %pad_maximum_fusion.a0), channel_id=1, source_target_pairs={{4,0},{6,2},{0,4},{2,6},{5,1},{7,3},{1,5},{3,7},{12,8},{14,10},{8,... | collective-permute-start | bytes 786440 | tf_op jit(solution)/shard_map/ppermute | solution.py:254
  19.4 10.2 %collective-permute-start.6 = (bf16[4,2,128,128]{3,2,1,0:T(8,128)(2,1)S(1)}, bf16[4,2,128,128]{3,2,1,0:T(8,128)(2,1)S(1)}, u32[]{:S(2)}, u32[]{:S(2)}) collective-permute-start(bf16[4,2,128,128]{3,2,1,0:T(8,128)(2,1)S(1)} %pad_maximum_fusion.a0), channel_id=1, source_target_pairs={{2,0},{4,2},{6,4},{0,6},{3,1},{5,3},{7,5},{1,7},{10,8},{12,10},{14... | collective-permute-start | bytes 786440 | tf_op jit(solution)/shard_map/ppermute | solution.py:254
  22.2 8.0 %collective-permute-start.2 = (bf16[8,64,128]{2,1,0:T(8,128)(2,1)S(1)}, bf16[8,64,128]{2,1,0:T(8,128)(2,1)S(1)}, u32[]{:S(2)}, u32[]{:S(2)}) collective-permute-start(bf16[8,64,128]{2,1,0:T(8,128)(2,1)S(1)} %all-to-all-done.q0), channel_id=1, source_target_pairs={{48,0},{0,16},{16,32},{32,48},{49,1},{1,17},{17,33},{33,49},{50,2}... | collective-permute-start | bytes 393224 | tf_op jit(solution)/shard_map/ppermute | solution.py:245
  23.7 7.1 %collective-permute-start.1 = (bf16[8,64,128]{2,1,0:T(8,128)(2,1)S(1)}, bf16[8,64,128]{2,1,0:T(8,128)(2,1)S(1)}, u32[]{:S(2)}, u32[]{:S(2)}) collective-permute-start(bf16[8,64,128]{2,1,0:T(8,128)(2,1)S(1)} %all-to-all-done.q0), channel_id=1, source_target_pairs={{32,0},{48,16},{0,32},{16,48},{33,1},{49,17},{1,33},{17,49},{34,2}... | collective-permute-start | bytes 393224 | tf_op jit(solution)/shard_map/ppermute | solution.py:245
  26.8 5.0 %collective-permute-start = (bf16[8,64,128]{2,1,0:T(8,128)(2,1)S(1)}, bf16[8,64,128]{2,1,0:T(8,128)(2,1)S(1)}, u32[]{:S(2)}, u32[]{:S(2)}) collective-permute-start(bf16[8,64,128]{2,1,0:T(8,128)(2,1)S(1)} %all-to-all-done.q0), channel_id=1, source_target_pairs={{16,0},{32,16},{48,32},{0,48},{17,1},{33,17},{49,33},{1,49},{18,2}... | collective-permute-start | bytes 393224 | tf_op jit(solution)/shard_map/ppermute | solution.py:245
  29.6 2.2 %collective-permute-start.9 = (bf16[4,2,128,128]{3,2,1,0:T(8,128)(2,1)S(1)}, bf16[4,2,128,128]{3,2,1,0:T(8,128)(2,1)S(1)}, u32[]{:S(2)}, u32[]{:S(2)}) collective-permute-start(bf16[4,2,128,128]{3,2,1,0:T(8,128)(2,1)S(1)} %pad_maximum_fusion.a0), channel_id=1, source_target_pairs={{0,1},{1,0},{2,3},{3,2},{4,5},{5,4},{6,7},{7,6},{8,9},{9,8},{10,11... | collective-permute-start | bytes 786440 | tf_op jit(solution)/shard_map/ppermute | solution.py:257
  29.7 2.2 %collective-permute-start.12 = (bf16[4,2,128,128]{3,2,1,0:T(8,128)(2,1)S(1)}, bf16[4,2,128,128]{3,2,1,0:T(8,128)(2,1)S(1)}, u32[]{:S(2)}, u32[]{:S(2)}) collective-permute-start(bf16[4,2,128,128]{3,2,1,0:T(8,128)(2,1)S(1)} %collective-permute-done.8.a3), channel_id=1, source_target_pairs={{0,1},{1,0},{2,3},{3,2},{4,5},{5,4},{6,7},{7,6},{8,9},{9,8},{10,11... | collective-permute-start | bytes 786440 | tf_op jit(solution)/shard_map/ppermute | solution.py:257
  30.2 1.8 %collective-permute-start.11 = (bf16[4,2,128,128]{3,2,1,0:T(8,128)(2,1)S(1)}, bf16[4,2,128,128]{3,2,1,0:T(8,128)(2,1)S(1)}, u32[]{:S(2)}, u32[]{:S(2)}) collective-permute-start(bf16[4,2,128,128]{3,2,1,0:T(8,128)(2,1)S(1)} %collective-permute-done.7.a2), channel_id=1, source_target_pairs={{0,1},{1,0},{2,3},{3,2},{4,5},{5,4},{6,7},{7,6},{8,9},{9,8},{10,11... | collective-permute-start | bytes 786440 | tf_op jit(solution)/shard_map/ppermute | solution.py:257
  30.8 1.5 %collective-permute-start.10 = (bf16[4,2,128,128]{3,2,1,0:T(8,128)(2,1)S(1)}, bf16[4,2,128,128]{3,2,1,0:T(8,128)(2,1)S(1)}, u32[]{:S(2)}, u32[]{:S(2)}) collective-permute-start(bf16[4,2,128,128]{3,2,1,0:T(8,128)(2,1)S(1)} %collective-permute-done.6.a1), channel_id=1, source_target_pairs={{0,1},{1,0},{2,3},{3,2},{4,5},{5,4},{6,7},{7,6},{8,9},{9,8},{10,11... | collective-permute-start | bytes 786440 | tf_op jit(solution)/shard_map/ppermute | solution.py:257
  38.6 7.2 %collective-permute-start.13 = (bf16[8,72,128]{2,1,0:T(8,128)(2,1)S(1)}, bf16[8,72,128]{2,1,0:T(8,128)(2,1)S(1)}, u32[]{:S(2)}, u32[]{:S(2)}) collective-permute-start(bf16[8,72,128]{2,1,0:T(8,128)(2,1)S(1)} %get-tuple-element.28), channel_id=1, source_target_pairs={{48,0},{0,16},{16,32},{32,48},{49,1},{1,17},{17,33},{33,49},{50,2}... | collective-permute-start | bytes 442376 | tf_op jit(solution)/shard_map/ppermute | solution.py:269
  40.1 9.9 %collective-permute-start.14 = (bf16[8,72,128]{2,1,0:T(8,128)(2,1)S(1)}, bf16[8,72,128]{2,1,0:T(8,128)(2,1)S(1)}, u32[]{:S(2)}, u32[]{:S(2)}) collective-permute-start(bf16[8,72,128]{2,1,0:T(8,128)(2,1)S(1)} %get-tuple-element.29), channel_id=1, source_target_pairs={{32,0},{48,16},{0,32},{16,48},{33,1},{49,17},{1,33},{17,49},{34,2}... | collective-permute-start | bytes 442376 | tf_op jit(solution)/shard_map/ppermute | solution.py:269
  43.0 7.0 %collective-permute-start.15 = (bf16[8,72,128]{2,1,0:T(8,128)(2,1)S(1)}, bf16[8,72,128]{2,1,0:T(8,128)(2,1)S(1)}, u32[]{:S(2)}, u32[]{:S(2)}) collective-permute-start(bf16[8,72,128]{2,1,0:T(8,128)(2,1)S(1)} %get-tuple-element.30), channel_id=1, source_target_pairs={{16,0},{32,16},{48,32},{0,48},{17,1},{33,17},{49,33},{1,49},{18,2}... | collective-permute-start | bytes 442376 | tf_op jit(solution)/shard_map/ppermute | solution.py:269

commit v4 on v3

--- a/solution.py
+++ b/solution.py
@@ -193,7 +193,7 @@
 
 def weighed(line, pick, rows):
     total = jnp.zeros((pick.shape[0], WIDTH), jnp.float32)
-    for piece in three_pieces(line):
+    for piece in three_pieces(line)[:2]:
         spread = jnp.where(pick, jnp.broadcast_to(piece, pick.shape), 0.0).astype(jnp.bfloat16)
         total = total + jnp.dot(spread, rows, preferred_element_type=jnp.float32)
     return total

time: 66.1 us -> 65.2 us (0.986)
  starting transfers between devices: 31 us -> 32.9 us
  blocking collectives: 14.1 us -> 12.5 us
  Pallas kernels: 8.32 us -> 6.8 us
    ppermute x3, starting transfers between devices: 5.74 us -> 7.64 us  [per_device(): lax.ppermute(part[k], 'x', turned(4 - k))]
    all_to_all x1, blocking collectives: 14.1 us -> 12.5 us  [per_device(): part = lax.all_to_all(part, ('zl', 'zh'), 0, 0, tiled=True)]
    pallas_call x1, Pallas kernels: 6.24 us -> 4.88 us  [attend_call(): pl.pallas_call(attend, out_shape=(jax.ShapeDtypeStruct((8, SLOT_ROWS, WID...]
where the time goes in v4:
time: 65.2 us; the launch traced here: 64.9 us
  starting transfers between devices  32.9 us (50%)
  blocking collectives  12.5 us (19%)
  waiting for transfers between devices  10.3 us (16%)
  Pallas kernels  6.8 us (10%)
  local copies, waits for them, and re-layouts  1.76 us (3%)
    all_to_all x1, blocking collectives, per_device(): part = lax.all_to_all(part, ('zl', 'zh'), 0, 0, tiled=True)  12.5 us
    all_to_all x1, starting transfers between devices, per_device(): q = lax.all_to_all(q, ('zl', 'zh'), 0, 0, tiled=True)  8.22 us
    ppermute x3, starting transfers between devices, per_device(): lax.ppermute(part[k], 'x', turned(4 - k))  7.64 us
    ppermute x3, starting transfers between devices, per_device(): a1, a2, a3 = (lax.ppermute(a0, 'y', turned(k)) for k in (1, 2, 3))  5.9 us
    ppermute x3, starting transfers between devices, per_device(): q = [q, *(lax.ppermute(q, 'x', turned(k)) for k in (1, 2, 3))]  5.73 us
    ppermute x3, waiting for transfers between devices, per_device(): lax.ppermute(part[k], 'x', turned(4 - k))  5.58 us
    pallas_call x1, Pallas kernels, attend_call(): pl.pallas_call(attend, out_shape=(jax.ShapeDtypeStruct((8, SLOT_ROWS, WID...  4.88 us
    ppermute x3, starting transfers between devices, per_device(): lax.ppermute(piece, 'zl', [(i, i ^ s) for i in range(4)])  4.82 us
  transfers between devices with their start and end apart: 17, of which 8 were waited for; matrix products, arithmetic and copies ran while one was open for 2% of the time, Pallas kernels for 0%

profile of v4, /device:TPU:32, one launch (start us, length us, event | category | flops | bytes accessed | tf_op | source)
XLA Modules:
  0.0 64.9 jit_solution(403272062811392128)
XLA Ops:
  0.0 0.9 %copy-done = bf16[2,128,512]{2,1,0:T(8,128)(2,1)S(1)} copy-done((bf16[2,128,512]{2,1,0:T(8,128)(2,1)S(1)}, bf16[2,128,512]{2,1,0:T(8,128)(2,1)}, u32[]{:S(2)}) %copy-start) | copy-done | bytes 262168
  1.0 2.0 %collective-permute-start.5 = (bf16[2,128,128]{2,1,0:T(8,128)(2,1)S(1)}, bf16[2,128,128]{2,1,0:T(8,128)(2,1)S(1)}, u32[]{:S(2)}, u32[]{:S(2)}) collective-permute-start(bf16[2,128,128]{2,1,0:T(8,128)(2,1)S(1)} %constant_dynamic-slice_fusion), channel_id=1, source_target_pairs={{0,192},{64,128},{128,64},{192,0},{1,193},{65,129},{129,65},{193,1... | collective-permute-start | bytes 196616 | tf_op jit(solution)/shard_map/ppermute | solution.py:251
  3.0 2.3 %collective-permute-start.4 = (bf16[2,128,128]{2,1,0:T(8,128)(2,1)S(1)}, bf16[2,128,128]{2,1,0:T(8,128)(2,1)S(1)}, u32[]{:S(2)}, u32[]{:S(2)}) collective-permute-start(bf16[2,128,128]{2,1,0:T(8,128)(2,1)S(1)} %constant_dynamic-slice_fusion.1), channel_id=1, source_target_pairs={{0,128},{64,192},{128,0},{192,64},{1,129},{65,193},{129,1},{193,65... | collective-permute-start | bytes 196616 | tf_op jit(solution)/shard_map/ppermute | solution.py:251
  5.3 0.5 collective-permute-start.3
  5.9 0.7 %broadcast_in_dim.32 = bf16[4,2,64,128]{3,2,1,0:T(8,128)(2,1)} broadcast(bf16[4,64,128]{2,1,0:T(8,128)(2,1)S(1)} %bitcast.17), dimensions={0,2,3} | broadcast | bytes 196608 | tf_op jit(solution)/shard_map/broadcast_in_dim | solution.py:243
  6.5 8.2 %all-to-all-start = ((bf16[8,64,128]{2,1,0:T(8,128)(2,1)}), bf16[8,64,128]{2,1,0:T(8,128)(2,1)S(1)}, u32[]{:S(2)}, u32[]{:S(2)}) async-start(bf16[8,64,128]{2,1,0:T(8,128)(2,1)} %bitcast.9), calls=%async_computation | async-start | bytes 262144 | tf_op jit(solution)/shard_map/all_to_all | solution.py:244
  14.9 1.7 %collective-permute-start.8 = (bf16[4,2,128,128]{3,2,1,0:T(8,128)(2,1)S(1)}, bf16[4,2,128,128]{3,2,1,0:T(8,128)(2,1)S(1)}, u32[]{:S(2)}, u32[]{:S(2)}) collective-permute-start(bf16[4,2,128,128]{3,2,1,0:T(8,128)(2,1)S(1)} %pad_maximum_fusion.a0), channel_id=1, source_target_pairs={{6,0},{0,2},{2,4},{4,6},{7,1},{1,3},{3,5},{5,7},{14,8},{8,10},{10,... | collective-permute-start | bytes 786440 | tf_op jit(solution)/shard_map/ppermute | solution.py:254
  16.5 2.9 %collective-permute-start.7 = (bf16[4,2,128,128]{3,2,1,0:T(8,128)(2,1)S(1)}, bf16[4,2,128,128]{3,2,1,0:T(8,128)(2,1)S(1)}, u32[]{:S(2)}, u32[]{:S(2)}) collective-permute-start(bf16[4,2,128,128]{3,2,1,0:T(8,128)(2,1)S(1)} %pad_maximum_fusion.a0), channel_id=1, source_target_pairs={{4,0},{6,2},{0,4},{2,6},{5,1},{7,3},{1,5},{3,7},{12,8},{14,10},{8,... | collective-permute-start | bytes 786440 | tf_op jit(solution)/shard_map/ppermute | solution.py:254
  19.4 1.3 %collective-permute-start.6 = (bf16[4,2,128,128]{3,2,1,0:T(8,128)(2,1)S(1)}, bf16[4,2,128,128]{3,2,1,0:T(8,128)(2,1)S(1)}, u32[]{:S(2)}, u32[]{:S(2)}) collective-permute-start(bf16[4,2,128,128]{3,2,1,0:T(8,128)(2,1)S(1)} %pad_maximum_fusion.a0), channel_id=1, source_target_pairs={{2,0},{4,2},{6,4},{0,6},{3,1},{5,3},{7,5},{1,7},{10,8},{12,10},{14... | collective-permute-start | bytes 786440 | tf_op jit(solution)/shard_map/ppermute | solution.py:254
  20.8 1.4 %all-to-all-done.q0 = bf16[8,64,128]{2,1,0:T(8,128)(2,1)S(1)} async-done(((bf16[8,64,128]{2,1,0:T(8,128)(2,1)}), bf16[8,64,128]{2,1,0:T(8,128)(2,1)S(1)}, u32[]{:S(2)}, u32[]{:S(2)}) %all-to-all-start) | async-done | bytes 131104 | tf_op jit(solution)/shard_map/all_to_all | solution.py:244
  22.2 1.5 %collective-permute-start.2 = (bf16[8,64,128]{2,1,0:T(8,128)(2,1)S(1)}, bf16[8,64,128]{2,1,0:T(8,128)(2,1)S(1)}, u32[]{:S(2)}, u32[]{:S(2)}) collective-permute-start(bf16[8,64,128]{2,1,0:T(8,128)(2,1)S(1)} %all-to-all-done.q0), channel_id=1, source_target_pairs={{48,0},{0,16},{16,32},{32,48},{49,1},{1,17},{17,33},{33,49},{50,2}... | collective-permute-start | bytes 393224 | tf_op jit(solution)/shard_map/ppermute | solution.py:245
  23.7 2.7 %collective-permute-start.1 = (bf16[8,64,128]{2,1,0:T(8,128)(2,1)S(1)}, bf16[8,64,128]{2,1,0:T(8,128)(2,1)S(1)}, u32[]{:S(2)}, u32[]{:S(2)}) collective-permute-start(bf16[8,64,128]{2,1,0:T(8,128)(2,1)S(1)} %all-to-all-done.q0), channel_id=1, source_target_pairs={{32,0},{48,16},{0,32},{16,48},{33,1},{49,17},{1,33},{17,49},{34,2}... | collective-permute-start | bytes 393224 | tf_op jit(solution)/shard_map/ppermute | solution.py:245
  26.4 0.2 select_reduce_fusion
  26.6 0.2 convert_reduce_fusion
  26.8 1.5 %collective-permute-start = (bf16[8,64,128]{2,1,0:T(8,128)(2,1)S(1)}, bf16[8,64,128]{2,1,0:T(8,128)(2,1)S(1)}, u32[]{:S(2)}, u32[]{:S(2)}) collective-permute-start(bf16[8,64,128]{2,1,0:T(8,128)(2,1)S(1)} %all-to-all-done.q0), channel_id=1, source_target_pairs={{16,0},{32,16},{48,32},{0,48},{17,1},{33,17},{49,33},{1,49},{18,2}... | collective-permute-start | bytes 393224 | tf_op jit(solution)/shard_map/ppermute | solution.py:245
  28.3 1.3 %collective-permute-done.7.a2 = bf16[4,2,128,128]{3,2,1,0:T(8,128)(2,1)S(1)} collective-permute-done((bf16[4,2,128,128]{3,2,1,0:T(8,128)(2,1)S(1)}, bf16[4,2,128,128]{3,2,1,0:T(8,128)(2,1)S(1)}, u32[]{:S(2)}, u32[]{:S(2)}) %collective-permute-start.7) | collective-permute-done | bytes 262176 | tf_op jit(solution)/shard_map/ppermute | solution.py:254
  29.7 0.5 collective-permute-start.12
  30.2 0.1 collective-permute-start.11
  30.3 0.5 collective-permute-done.1.q2
  30.8 0.1 concatenate.3.scal
  30.9 1.0 %collective-permute-done.q1 = bf16[8,64,128]{2,1,0:T(8,128)(2,1)S(1)} collective-permute-done((bf16[8,64,128]{2,1,0:T(8,128)(2,1)S(1)}, bf16[8,64,128]{2,1,0:T(8,128)(2,1)S(1)}, u32[]{:S(2)}, u32[]{:S(2)}) %collective-permute-start) | collective-permute-done | bytes 131104 | tf_op jit(solution)/shard_map/ppermute | solution.py:245
  31.8 0.1 collective-permute-done.11.b2
  31.9 0.4 collective-permute-done.10.b1
  32.3 4.9 %attend.1 = (bf16[8,72,128]{2,1,0:T(8,128)(2,1)S(1)}, bf16[8,72,128]{2,1,0:T(8,128)(2,1)S(1)}, bf16[8,72,128]{2,1,0:T(8,128)(2,1)S(1)}, bf16[8,72,128]{2,1,0:T(8,128)(2,1)S(1)}) custom-call(s32[30]{0:T(128)S(1)} %concatenate.3.scal, bf16[8,64,128]{2,1,0:T(8,128)(2,1)S(1)} %all-to-all-done.q0, bf16[8,64,128]{2,1,0:T(8,128)(2,1)S(1)} %collective-permute-done.q1, ...), custom_call_target="tpu_custom_call" | custom-call | tf_op jit(solution)/shard_map/attend/pallas_call | solution.py:162
  37.2 1.6 %collective-permute-start.13 = (bf16[8,72,128]{2,1,0:T(8,128)(2,1)S(1)}, bf16[8,72,128]{2,1,0:T(8,128)(2,1)S(1)}, u32[]{:S(2)}, u32[]{:S(2)}) collective-permute-start(bf16[8,72,128]{2,1,0:T(8,128)(2,1)S(1)} %get-tuple-element.28), channel_id=1, source_target_pairs={{48,0},{0,16},{16,32},{32,48},{49,1},{1,17},{17,33},{33,49},{50,2}... | collective-permute-start | bytes 442376 | tf_op jit(solution)/shard_map/ppermute | solution.py:269
  38.8 4.6 %collective-permute-start.14 = (bf16[8,72,128]{2,1,0:T(8,128)(2,1)S(1)}, bf16[8,72,128]{2,1,0:T(8,128)(2,1)S(1)}, u32[]{:S(2)}, u32[]{:S(2)}) collective-permute-start(bf16[8,72,128]{2,1,0:T(8,128)(2,1)S(1)} %get-tuple-element.29), channel_id=1, source_target_pairs={{32,0},{48,16},{0,32},{16,48},{33,1},{49,17},{1,33},{17,49},{34,2}... | collective-permute-start | bytes 442376 | tf_op jit(solution)/shard_map/ppermute | solution.py:269
  43.4 1.4 %collective-permute-start.15 = (bf16[8,72,128]{2,1,0:T(8,128)(2,1)S(1)}, bf16[8,72,128]{2,1,0:T(8,128)(2,1)S(1)}, u32[]{:S(2)}, u32[]{:S(2)}) collective-permute-start(bf16[8,72,128]{2,1,0:T(8,128)(2,1)S(1)} %get-tuple-element.30), channel_id=1, source_target_pairs={{16,0},{32,16},{48,32},{0,48},{17,1},{33,17},{49,33},{1,49},{18,2}... | collective-permute-start | bytes 442376 | tf_op jit(solution)/shard_map/ppermute | solution.py:269
  44.8 1.2 %collective-permute-done.13.p1 = bf16[8,72,128]{2,1,0:T(8,128)(2,1)S(1)} collective-permute-done((bf16[8,72,128]{2,1,0:T(8,128)(2,1)S(1)}, bf16[8,72,128]{2,1,0:T(8,128)(2,1)S(1)}, u32[]{:S(2)}, u32[]{:S(2)}) %collective-permute-start.13) | collective-permute-done | bytes 147488 | tf_op jit(solution)/shard_map/ppermute | solution.py:269
  46.1 4.3 %collective-permute-done.14.p2 = bf16[8,72,128]{2,1,0:T(8,128)(2,1)S(1)} collective-permute-done((bf16[8,72,128]{2,1,0:T(8,128)(2,1)S(1)}, bf16[8,72,128]{2,1,0:T(8,128)(2,1)S(1)}, u32[]{:S(2)}, u32[]{:S(2)}) %collective-permute-start.14) | collective-permute-done | bytes 147488 | tf_op jit(solution)/shard_map/ppermute | solution.py:269
  50.4 0.4 merge.1
  50.9 12.5 %all_to_all.10.parts = bf16[8,72,128]{2,1,0:T(8,128)(2,1)S(1)} all-to-all(bf16[8,72,128]{2,1,0:T(8,128)(2,1)S(1)} %merge.1), channel_id=1, replica_groups=mesh['zl'=4,'x'=4,'zh'=2,'y'=4,'core'=2] {'zl','zh'}, dimensions={0} | all-to-all | bytes 294912 | tf_op jit(solution)/shard_map/all_to_all | solution.py:278
  63.4 1.5 %combine.1 = bf16[4,8192]{1,0:T(4,128)(2,1)} custom-call(s32[30]{0:T(128)S(1)} %concatenate.3.scal, bf16[8,72,128]{2,1,0:T(8,128)(2,1)S(1)} %all_to_all.10.parts), custom_call_target="tpu_custom_call" | custom-call | tf_op jit(solution)/shard_map/combine/pallas_call | solution.py:279
  (24 shorter events, 0.2 us)
Async XLA Ops:
  0.0 1.0 %copy-start = (bf16[2,128,512]{2,1,0:T(8,128)(2,1)S(1)}, bf16[2,128,512]{2,1,0:T(8,128)(2,1)}, u32[]{:S(2)}) copy-start(bf16[2,128,512]{2,1,0:T(8,128)(2,1)} %param.4) | copy-start | bytes 786436
  1.0 4.9 %copy-start.1 = (bf16[4,8192]{1,0:T(4,128)(2,1)S(1)}, bf16[4,8192]{1,0:T(4,128)(2,1)}, u32[]{:S(2)}) copy-start(bf16[4,8192]{1,0:T(4,128)(2,1)} %param.3) | copy-start | bytes 196612
  1.0 13.7 %collective-permute-start.5 = (bf16[2,128,128]{2,1,0:T(8,128)(2,1)S(1)}, bf16[2,128,128]{2,1,0:T(8,128)(2,1)S(1)}, u32[]{:S(2)}, u32[]{:S(2)}) collective-permute-start(bf16[2,128,128]{2,1,0:T(8,128)(2,1)S(1)} %constant_dynamic-slice_fusion), channel_id=1, source_target_pairs={{0,192},{64,128},{128,64},{192,0},{1,193},{65,129},{129,65},{193,1... | collective-permute-start | bytes 196616 | tf_op jit(solution)/shard_map/ppermute | solution.py:251
  3.0 11.7 %collective-permute-start.4 = (bf16[2,128,128]{2,1,0:T(8,128)(2,1)S(1)}, bf16[2,128,128]{2,1,0:T(8,128)(2,1)S(1)}, u32[]{:S(2)}, u32[]{:S(2)}) collective-permute-start(bf16[2,128,128]{2,1,0:T(8,128)(2,1)S(1)} %constant_dynamic-slice_fusion.1), channel_id=1, source_target_pairs={{0,128},{64,192},{128,0},{192,64},{1,129},{65,193},{129,1},{193,65... | collective-permute-start | bytes 196616 | tf_op jit(solution)/shard_map/ppermute | solution.py:251
  5.3 9.5 %collective-permute-start.3 = (bf16[2,128,128]{2,1,0:T(8,128)(2,1)S(1)}, bf16[2,128,128]{2,1,0:T(8,128)(2,1)S(1)}, u32[]{:S(2)}, u32[]{:S(2)}) collective-permute-start(bf16[2,128,128]{2,1,0:T(8,128)(2,1)S(1)} %constant_dynamic-slice_fusion.2), channel_id=1, source_target_pairs={{0,64},{64,0},{128,192},{192,128},{1,65},{65,1},{129,193},{193,129... | collective-permute-start | bytes 196616 | tf_op jit(solution)/shard_map/ppermute | solution.py:251
  6.5 15.7 %all-to-all-start = ((bf16[8,64,128]{2,1,0:T(8,128)(2,1)}), bf16[8,64,128]{2,1,0:T(8,128)(2,1)S(1)}, u32[]{:S(2)}, u32[]{:S(2)}) async-start(bf16[8,64,128]{2,1,0:T(8,128)(2,1)} %bitcast.9), calls=%async_computation | async-start | bytes 262144 | tf_op jit(solution)/shard_map/all_to_all | solution.py:244
  14.8 11.6 %copy-start.2 = (s32[256]{0:T(256)S(1)}, s32[256]{0:T(256)}, u32[]{:S(2)}) copy-start(s32[256]{0:T(256)} %param.5) | copy-start | bytes 3076
  14.9 11.9 %collective-permute-start.8 = (bf16[4,2,128,128]{3,2,1,0:T(8,128)(2,1)S(1)}, bf16[4,2,128,128]{3,2,1,0:T(8,128)(2,1)S(1)}, u32[]{:S(2)}, u32[]{:S(2)}) collective-permute-start(bf16[4,2,128,128]{3,2,1,0:T(8,128)(2,1)S(1)} %pad_maximum_fusion.a0), channel_id=1, source_target_pairs={{6,0},{0,2},{2,4},{4,6},{7,1},{1,3},{3,5},{5,7},{14,8},{8,10},{10,... | collective-permute-start | bytes 786440 | tf_op jit(solution)/shard_map/ppermute | solution.py:254
  16.5 13.1 %collective-permute-start.7 = (bf16[4,2,128,128]{3,2,1,0:T(8,128)(2,1)S(1)}, bf16[4,2,128,128]{3,2,1,0:T(8,128)(2,1)S(1)}, u32[]{:S(2)}, u32[]{:S(2)}) collective-permute-start(bf16[4,2,128,128]{3,2,1,0:T(8,128)(2,1)S(1)} %pad_maximum_fusion.a0), channel_id=1, source_target_pairs={{4,0},{6,2},{0,4},{2,6},{5,1},{7,3},{1,5},{3,7},{12,8},{14,10},{8,... | collective-permute-start | bytes 786440 | tf_op jit(solution)/shard_map/ppermute | solution.py:254
  19.4 10.2 %collective-permute-start.6 = (bf16[4,2,128,128]{3,2,1,0:T(8,128)(2,1)S(1)}, bf16[4,2,128,128]{3,2,1,0:T(8,128)(2,1)S(1)}, u32[]{:S(2)}, u32[]{:S(2)}) collective-permute-start(bf16[4,2,128,128]{3,2,1,0:T(8,128)(2,1)S(1)} %pad_maximum_fusion.a0), channel_id=1, source_target_pairs={{2,0},{4,2},{6,4},{0,6},{3,1},{5,3},{7,5},{1,7},{10,8},{12,10},{14... | collective-permute-start | bytes 786440 | tf_op jit(solution)/shard_map/ppermute | solution.py:254
  22.2 8.0 %collective-permute-start.2 = (bf16[8,64,128]{2,1,0:T(8,128)(2,1)S(1)}, bf16[8,64,128]{2,1,0:T(8,128)(2,1)S(1)}, u32[]{:S(2)}, u32[]{:S(2)}) collective-permute-start(bf16[8,64,128]{2,1,0:T(8,128)(2,1)S(1)} %all-to-all-done.q0), channel_id=1, source_target_pairs={{48,0},{0,16},{16,32},{32,48},{49,1},{1,17},{17,33},{33,49},{50,2}... | collective-permute-start | bytes 393224 | tf_op jit(solution)/shard_map/ppermute | solution.py:245
  23.7 7.1 %collective-permute-start.1 = (bf16[8,64,128]{2,1,0:T(8,128)(2,1)S(1)}, bf16[8,64,128]{2,1,0:T(8,128)(2,1)S(1)}, u32[]{:S(2)}, u32[]{:S(2)}) collective-permute-start(bf16[8,64,128]{2,1,0:T(8,128)(2,1)S(1)} %all-to-all-done.q0), channel_id=1, source_target_pairs={{32,0},{48,16},{0,32},{16,48},{33,1},{49,17},{1,33},{17,49},{34,2}... | collective-permute-start | bytes 393224 | tf_op jit(solution)/shard_map/ppermute | solution.py:245
  26.8 5.0 %collective-permute-start = (bf16[8,64,128]{2,1,0:T(8,128)(2,1)S(1)}, bf16[8,64,128]{2,1,0:T(8,128)(2,1)S(1)}, u32[]{:S(2)}, u32[]{:S(2)}) collective-permute-start(bf16[8,64,128]{2,1,0:T(8,128)(2,1)S(1)} %all-to-all-done.q0), channel_id=1, source_target_pairs={{16,0},{32,16},{48,32},{0,48},{17,1},{33,17},{49,33},{1,49},{18,2}... | collective-permute-start | bytes 393224 | tf_op jit(solution)/shard_map/ppermute | solution.py:245
  29.6 2.2 %collective-permute-start.9 = (bf16[4,2,128,128]{3,2,1,0:T(8,128)(2,1)S(1)}, bf16[4,2,128,128]{3,2,1,0:T(8,128)(2,1)S(1)}, u32[]{:S(2)}, u32[]{:S(2)}) collective-permute-start(bf16[4,2,128,128]{3,2,1,0:T(8,128)(2,1)S(1)} %pad_maximum_fusion.a0), channel_id=1, source_target_pairs={{0,1},{1,0},{2,3},{3,2},{4,5},{5,4},{6,7},{7,6},{8,9},{9,8},{10,11... | collective-permute-start | bytes 786440 | tf_op jit(solution)/shard_map/ppermute | solution.py:257
  29.7 2.2 %collective-permute-start.12 = (bf16[4,2,128,128]{3,2,1,0:T(8,128)(2,1)S(1)}, bf16[4,2,128,128]{3,2,1,0:T(8,128)(2,1)S(1)}, u32[]{:S(2)}, u32[]{:S(2)}) collective-permute-start(bf16[4,2,128,128]{3,2,1,0:T(8,128)(2,1)S(1)} %collective-permute-done.8.a3), channel_id=1, source_target_pairs={{0,1},{1,0},{2,3},{3,2},{4,5},{5,4},{6,7},{7,6},{8,9},{9,8},{10,11... | collective-permute-start | bytes 786440 | tf_op jit(solution)/shard_map/ppermute | solution.py:257
  30.2 1.8 %collective-permute-start.11 = (bf16[4,2,128,128]{3,2,1,0:T(8,128)(2,1)S(1)}, bf16[4,2,128,128]{3,2,1,0:T(8,128)(2,1)S(1)}, u32[]{:S(2)}, u32[]{:S(2)}) collective-permute-start(bf16[4,2,128,128]{3,2,1,0:T(8,128)(2,1)S(1)} %collective-permute-done.7.a2), channel_id=1, source_target_pairs={{0,1},{1,0},{2,3},{3,2},{4,5},{5,4},{6,7},{7,6},{8,9},{9,8},{10,11... | collective-permute-start | bytes 786440 | tf_op jit(solution)/shard_map/ppermute | solution.py:257
  30.8 1.5 %collective-permute-start.10 = (bf16[4,2,128,128]{3,2,1,0:T(8,128)(2,1)S(1)}, bf16[4,2,128,128]{3,2,1,0:T(8,128)(2,1)S(1)}, u32[]{:S(2)}, u32[]{:S(2)}) collective-permute-start(bf16[4,2,128,128]{3,2,1,0:T(8,128)(2,1)S(1)} %collective-permute-done.6.a1), channel_id=1, source_target_pairs={{0,1},{1,0},{2,3},{3,2},{4,5},{5,4},{6,7},{7,6},{8,9},{9,8},{10,11... | collective-permute-start | bytes 786440 | tf_op jit(solution)/shard_map/ppermute | solution.py:257
  37.2 8.9 %collective-permute-start.13 = (bf16[8,72,128]{2,1,0:T(8,128)(2,1)S(1)}, bf16[8,72,128]{2,1,0:T(8,128)(2,1)S(1)}, u32[]{:S(2)}, u32[]{:S(2)}) collective-permute-start(bf16[8,72,128]{2,1,0:T(8,128)(2,1)S(1)} %get-tuple-element.28), channel_id=1, source_target_pairs={{48,0},{0,16},{16,32},{32,48},{49,1},{1,17},{17,33},{33,49},{50,2}... | collective-permute-start | bytes 442376 | tf_op jit(solution)/shard_map/ppermute | solution.py:269
  38.8 11.7 %collective-permute-start.14 = (bf16[8,72,128]{2,1,0:T(8,128)(2,1)S(1)}, bf16[8,72,128]{2,1,0:T(8,128)(2,1)S(1)}, u32[]{:S(2)}, u32[]{:S(2)}) collective-permute-start(bf16[8,72,128]{2,1,0:T(8,128)(2,1)S(1)} %get-tuple-element.29), channel_id=1, source_target_pairs={{32,0},{48,16},{0,32},{16,48},{33,1},{49,17},{1,33},{17,49},{34,2}... | collective-permute-start | bytes 442376 | tf_op jit(solution)/shard_map/ppermute | solution.py:269
  43.4 7.0 %collective-permute-start.15 = (bf16[8,72,128]{2,1,0:T(8,128)(2,1)S(1)}, bf16[8,72,128]{2,1,0:T(8,128)(2,1)S(1)}, u32[]{:S(2)}, u32[]{:S(2)}) collective-permute-start(bf16[8,72,128]{2,1,0:T(8,128)(2,1)S(1)} %get-tuple-element.30), channel_id=1, source_target_pairs={{16,0},{32,16},{48,32},{0,48},{17,1},{33,17},{49,33},{1,49},{18,2}... | collective-permute-start | bytes 442376 | tf_op jit(solution)/shard_map/ppermute | solution.py:269
